TPU v7x, 256 devices: a whole 4x4x8 slice. The times are simulated.
256 devices in a mesh: ax: 4 (over y_hi, core), az: 64 (over y_lo, x, z).
Axes of the slice: x: 4, y: 4 (y_hi: 2, y_lo: 2; y = y_hi * 2 + y_lo), z: 8, core: 2. Of those that a mesh axis runs over, the one named last changes fastest.
Arguments:
- state: float32 [5, 16, 2560, 128], P(None, 'ax', 'az'), may hold values from -4 to 8, as said below
- shock_flags: int32 [2, 16, 2560, 128], P(None, 'ax', 'az'), may hold values from 0 to 1
Outputs:
- increment: float32 [5, 16, 2560, 128], P(None, 'ax', 'az')
Inputs may be any that keep to these rules, and one draw needn't show every extreme that they name: `state`: density in 0.8 to 1.25 and pressure in 0.8 to 1.25 in every cell.
All inputs are finite; a program needn't handle non-finite values.
Results may differ from a plain program's by a relative error of at most 0.0003.
Values sent between devices are 32-bit elements; how exact they have to be, the bound alone decides.
A program may use at most 64 MiB of HBM per device.

v0:
```python
import math

import jax
import jax.numpy as jnp
import numpy as np
from jax import lax
from jax.experimental import pallas as pl
from jax.experimental.pallas import tpu as pltpu
from jax.sharding import PartitionSpec as P

NRING = 16
KEEP = 32


split_speed = 3.0
small_eps = 1e-06
time_step = 0.004


def with_halo(shard, sides, width):
    for axis, dim in sides:
        devices, length = (lax.axis_size(axis), shard.shape[dim])
        up = [(i, (i + 1) % devices) for i in range(devices)]
        down = [(j, i) for i, j in up]
        last = lax.slice_in_dim(shard, length - width, length, axis=dim)
        leading = lax.slice_in_dim(shard, 0, width, axis=dim)
        before = lax.ppermute(last, axis, up)
        after = lax.ppermute(leading, axis, down)
        shard = jnp.concatenate([before, shard, after], axis=dim)
    return shard


def passed_along(shard, axis, by):
    devices = lax.axis_size(axis)
    return lax.ppermute(shard, axis, [(i, (i + by) % devices) for i in range(devices)])


def pressure_of(conserved):
    return 0.4 * (
        conserved[4]
        - 0.5
        * (conserved[1] * conserved[1] + conserved[2] * conserved[2] + conserved[3] * conserved[3])
        / conserved[0]
    )


def euler_flux(conserved, component):
    velocity = conserved[1 + component] / conserved[0]
    pressure = pressure_of(conserved)
    parts = [
        conserved[0] * velocity,
        conserved[1] * velocity,
        conserved[2] * velocity,
        conserved[3] * velocity,
        (conserved[4] + pressure) * velocity,
    ]
    parts[1 + component] = parts[1 + component] + pressure
    return jnp.stack(parts)


def weno_side(far_left, left, centre, right, far_right):
    cand_zero = (2.0 * far_left - 7.0 * left + 11.0 * centre) / 6.0
    cand_one = (-left + 5.0 * centre + 2.0 * right) / 6.0
    cand_two = (2.0 * centre + 5.0 * right - far_right) / 6.0
    smooth_zero = (
        13.0 / 12.0 * (far_left - 2.0 * left + centre) ** 2
        + 0.25 * (far_left - 4.0 * left + 3.0 * centre) ** 2
    )
    smooth_one = 13.0 / 12.0 * (left - 2.0 * centre + right) ** 2 + 0.25 * (left - right) ** 2
    smooth_two = (
        13.0 / 12.0 * (centre - 2.0 * right + far_right) ** 2
        + 0.25 * (3.0 * centre - 4.0 * right + far_right) ** 2
    )
    weight_zero = 0.1 / (small_eps + smooth_zero) ** 2
    weight_one = 0.6 / (small_eps + smooth_one) ** 2
    weight_two = 0.3 / (small_eps + smooth_two) ** 2
    return (weight_zero * cand_zero + weight_one * cand_one + weight_two * cand_two) / (
        weight_zero + weight_one + weight_two
    )


def face_flux(conserved, flag_field, axis_dim, cell_count, component):
    fluxes = euler_flux(conserved, component)
    plus_part = 0.5 * (fluxes + split_speed * conserved)
    minus_part = 0.5 * (fluxes - split_speed * conserved)

    def take(field, offset, along):
        return lax.slice_in_dim(field, 2 + offset, 3 + offset + cell_count, axis=along)

    plus_face = weno_side(
        take(plus_part, -2, axis_dim),
        take(plus_part, -1, axis_dim),
        take(plus_part, 0, axis_dim),
        take(plus_part, 1, axis_dim),
        take(plus_part, 2, axis_dim),
    )
    minus_face = weno_side(
        take(minus_part, 3, axis_dim),
        take(minus_part, 2, axis_dim),
        take(minus_part, 1, axis_dim),
        take(minus_part, 0, axis_dim),
        take(minus_part, -1, axis_dim),
    )
    central = (
        -take(fluxes, -1, axis_dim)
        + 7.0 * take(fluxes, 0, axis_dim)
        + 7.0 * take(fluxes, 1, axis_dim)
        - take(fluxes, 2, axis_dim)
    ) / 12.0
    switch = take(flag_field, -2, axis_dim - 1)
    for offset in range(-1, 4):
        switch = jnp.maximum(switch, take(flag_field, offset, axis_dim - 1))
    return jnp.where(switch[None] > 0.5, plus_face + minus_face, central)


def tendency(strip_axial, strip_turn, ghost, dtheta):
    axial_n = strip_axial.shape[1] - 6
    turn_n = strip_turn.shape[2] - 6
    axial_faces = face_flux(strip_axial[:5], strip_axial[5], 1, axial_n, 0)
    axial_diff = axial_faces[:, 1:] - axial_faces[:, :-1]
    turn_faces = face_flux(strip_turn[:5], strip_turn[5], 2, turn_n, 2)
    turn_diff = turn_faces[:, :, 1:] - turn_faces[:, :, :-1]
    inner = strip_turn[:5, :, 3 : 3 + turn_n]
    radial = euler_flux(inner, 1)
    radial_ghost = euler_flux(ghost[..., None], 1)
    radial_pad = jnp.concatenate([radial_ghost, radial, radial[..., -1:]], axis=3)
    radial_diff = 0.5 * (radial_pad[..., 2:] - radial_pad[..., :-2])
    swirl = inner[3] / inner[0]
    pressure = pressure_of(inner)
    zeros_field = jnp.zeros_like(pressure)
    source = jnp.stack(
        [zeros_field, zeros_field, inner[3] * swirl + pressure, -inner[2] * swirl, zeros_field]
    )
    radius = jnp.arange(inner.shape[3], dtype=jnp.float32) + 0.5
    return -axial_diff - radial_diff - (radial - source) / radius - turn_diff / (radius * dtheta)


def filter_tables():
    d, k1 = np.arange(64), np.arange(33)
    angle = 2 * np.pi * np.outer(k1, d) / 64
    fwd = np.zeros((80, 64))
    fwd[:33], fwd[40:73] = np.cos(angle), -np.sin(angle)
    inv = np.zeros((64, 80))
    inv[:, :33], inv[:, 40:73] = np.cos(angle.T), -np.sin(angle.T)
    twiddle = np.zeros((4, 40, 256))
    m_in, m_out = np.arange(40), np.arange(-3, 43)
    scale = np.where((k1 == 0) | (k1 == 32), 1.0, 2.0)[:, None] / 2560
    for v in range(5):
        angle = 2 * np.pi * np.outer(k1, m_in) / 2560
        twiddle[0, :33, v * 40 : v * 40 + 40] = np.cos(angle)
        twiddle[1, :33, v * 40 : v * 40 + 40] = -np.sin(angle)
        angle = 2 * np.pi * np.outer(k1, m_out) / 2560
        twiddle[2, :33, v * 46 : v * 46 + 46] = np.cos(angle) * scale
        twiddle[3, :33, v * 46 : v * 46 + 46] = np.sin(angle) * scale
    band = np.zeros((16, 4, 40, 256))
    delta = m_out[None, :] - m_in[:, None]
    for j in range(16):
        if j % 2:
            q = (j + 1) // 2
            modes, extra = np.arange(-q, q), -q
        else:
            q = j // 2
            modes, extra = np.arange(-q, q + 1), q
        kept = sum(np.exp(2j * np.pi * k * delta / 40) for k in modes)
        twin = np.exp(2j * np.pi * extra * delta / 40)
        band[j, 0, :, :46], band[j, 1, :, :46] = kept.real, kept.imag
        band[j, 2, :, :46], band[j, 3, :, :46] = twin.real, twin.imag
    return [a.astype(np.float32) for a in (fwd, inv, twiddle, band)]


def matmul(a, b):
    return jnp.dot(a, b, precision=lax.Precision.HIGHEST, preferred_element_type=jnp.float32)


def spread(send, recv, me, send_sem, recv_sem):
    def one(i, carry):
        to = lax.rem(me + i, 64)
        pltpu.make_async_remote_copy(
            src_ref=send.at[to],
            dst_ref=recv.at[me],
            send_sem=send_sem,
            recv_sem=recv_sem,
            device_id={"az": to},
            device_id_type=pl.DeviceIdType.MESH,
        ).start()
        return carry

    lax.fori_loop(1, 64, one, 0)
    recv[pl.ds(me, 1)] = send[pl.ds(me, 1)]


def arrived(buffer, sem):
    rows = buffer.at[pl.ds(0, 63)]
    pltpu.make_async_copy(rows, rows, sem).wait()


def filter_kernel(
    lines, fwd, inv, twiddle, band, out, send, recv, back, ret, mine, mix, send_sem, recv_sem, sem
):
    me = lax.axis_index("az")
    load = pltpu.make_async_copy(band.at[lax.rem(me, 16)], mine, sem)
    load.start()
    barrier = pltpu.get_barrier_semaphore()

    def greet(i, carry):
        pl.semaphore_signal(
            barrier,
            inc=1,
            device_id={"az": lax.rem(me + i, 64)},
            device_id_type=pl.DeviceIdType.MESH,
        )
        return carry

    lax.fori_loop(1, 64, greet, 0)
    send[:, 0, :] = lines[:, :128]
    send[:, 1, :] = lines[:, 128:]
    pl.semaphore_wait(barrier, 63)
    spread(send, recv, me, send_sem.at[0], recv_sem.at[0])
    load.wait()
    mix[...] = jnp.zeros_like(mix)
    for part in range(2):
        re, im = mine[2 * part], mine[2 * part + 1]
        for v in range(5):
            c = pltpu.roll(re, 46 * v, 1) if v else re
            s = pltpu.roll(im, 46 * v, 1) if v else im
            row = 512 * part + 40 * v
            mix[row : row + 40, :256] = c
            mix[row : row + 40, 256:] = s
            mix[row + 256 : row + 296, :256] = -s
            mix[row + 256 : row + 296, 256:] = c
    arrived(recv, recv_sem.at[0])
    x = jnp.concatenate([recv[:, 0, :], recv[:, 1, :]], axis=1)
    a = matmul(fwd[...], x)
    re, im = a[:40], a[40:]
    re, im = re * twiddle[0] - im * twiddle[1], re * twiddle[1] + im * twiddle[0]
    special = jnp.where(lax.rem(me, 2) == 1, 0, 32)
    own = (lax.broadcasted_iota(jnp.int32, (40, 256), 0) == special).astype(jnp.float32)
    z = matmul(jnp.concatenate([re, im, re * own, im * own], axis=1), mix[...])
    re, im = z[:, :256], z[:, 256:]
    re, im = re * twiddle[2] - im * twiddle[3], re * twiddle[3] + im * twiddle[2]
    y = matmul(inv[...], jnp.concatenate([re, im], axis=0))
    back[:, 0, :] = y[:, :128]
    back[:, 1, :] = y[:, 128:]
    spread(back, ret, me, send_sem.at[1], recv_sem.at[1])
    arrived(ret, recv_sem.at[1])
    out[:, :128] = ret[:, 0, :]
    out[:, 128:] = ret[:, 1, :]
    arrived(send, send_sem.at[0])
    arrived(back, send_sem.at[1])


def cycle_filter(conserved, tables, collective):
    cycles = conserved[..., :NRING]
    lines = jnp.transpose(cycles, (1, 3, 0, 2)).reshape(64, 200)
    lines = jnp.pad(lines, ((0, 0), (0, 56)))
    vmem = pl.BlockSpec(memory_space=pltpu.VMEM)
    message = pltpu.VMEM((64, 2, 128), jnp.float32)
    smooth = pl.pallas_call(
        filter_kernel,
        out_shape=jax.ShapeDtypeStruct((64, 256), jnp.float32),
        in_specs=[vmem] * 4 + [pl.BlockSpec(memory_space=pl.ANY)],
        out_specs=vmem,
        scratch_shapes=[
            message,
            message,
            message,
            message,
            pltpu.VMEM((4, 40, 256), jnp.float32),
            pltpu.VMEM((1024, 512), jnp.float32),
            pltpu.SemaphoreType.DMA((2,)),
            pltpu.SemaphoreType.DMA((2,)),
            pltpu.SemaphoreType.DMA,
        ],
        compiler_params=pltpu.CompilerParams(
            collective_id=collective, has_side_effects=True, vmem_limit_bytes=48 * 1024 * 1024
        ),
    )(lines, *tables)
    smooth = smooth[:, :230].reshape(4, NRING, 5, 46)[..., 3:43]
    smooth_cycles = jnp.transpose(smooth, (2, 0, 3, 1))
    return jnp.concatenate([smooth_cycles, conserved[..., NRING:]], axis=3)


def section_rate(conserved, flags):
    turn_n = conserved.shape[2]
    signs = jnp.array([1.0, 1.0, -1.0, -1.0, 1.0], dtype=jnp.float32)[:, None, None]
    stacked = jnp.concatenate([conserved, flags.astype(jnp.float32)[None]], axis=0)
    padded = with_halo(stacked, (("ax", 1), ("az", 2)), 3)
    strip_axial = padded[:, :, 3 : 3 + turn_n]
    strip_turn = padded[:, 3:-3]
    device_row = lax.axis_index("ax")
    last_row = lax.axis_size("ax") - 1
    lower_rim = jnp.broadcast_to(
        strip_axial[:, 3:4], (strip_axial.shape[0], 3) + strip_axial.shape[2:]
    )
    upper_rim = jnp.broadcast_to(
        strip_axial[:, -4:-3], (strip_axial.shape[0], 3) + strip_axial.shape[2:]
    )
    strip_axial = jnp.concatenate(
        [
            jnp.where(device_row == 0, lower_rim, strip_axial[:, :3]),
            strip_axial[:, 3:-3],
            jnp.where(device_row == last_row, upper_rim, strip_axial[:, -3:]),
        ],
        axis=1,
    )
    ghost = passed_along(conserved[:, :, :, 0] * signs, "az", lax.axis_size("az") // 2)
    return tendency(strip_axial, strip_turn, ghost, 2.0 * math.pi / (turn_n * lax.axis_size("az")))


def local(state, shock_flags):
    tables = [jnp.asarray(t) for t in filter_tables()]
    first = cycle_filter(state + time_step * section_rate(state, shock_flags[0]), tables, 0)
    second = cycle_filter(
        0.75 * state + 0.25 * (first + time_step * section_rate(first, shock_flags[1])), tables, 1
    )
    return second - state


def solution(mesh):
    in_specs = (P(None, "ax", "az", None), P(None, "ax", "az", None))
    out_specs = P(None, "ax", "az", None)
    return jax.shard_map(local, mesh=mesh, in_specs=in_specs, out_specs=out_specs, check_vma=False)
```

profile of v0, /device:TPU:1, one launch (start us, length us, event | category | flops | bytes accessed | tf_op | source)
XLA Modules:
  0.0 128.9 jit_solution(10485092811685381049)
XLA Ops:
  0.0 1.3 copy.39
  2.0 2.1 %collective-permute-start.2 = (f32[5,4,40]{2,1,0:T(4,128)S(1)}, f32[5,4,40]{2,1,0:T(4,128)S(1)}, u32[]{:S(2)}, u32[]{:S(2)}) collective-permute-start(f32[5,4,40]{2,1,0:T(4,128)S(1)} %bitcast_multiply_fusion), channel_id=1, source_target_pairs={{0,32},{1,33},{2,34},{3,35},{4,36},{5,37},{6,38},{7,39},{8,40},{9,... | collective-permute-start | bytes 9608 | tf_op jit(solution)/shard_map/ppermute | solution.py:35
  5.1 1.1 fusion.42
  6.2 3.5 %collective-permute-start = (f32[6,3,40,128]{3,2,1,0:T(8,128)S(1)}, f32[6,3,40,128]{3,2,1,0:T(8,128)S(1)}, u32[]{:S(2)}, u32[]{:S(2)}) collective-permute-start(f32[6,3,40,128]{3,2,1,0:T(8,128)S(1)} %get-tuple-element.68), channel_id=1, source_target_pairs={{0,64},{64,128},{128,192},{192,0},{1,65},{65,129},{129,193},{193,1... | collective-permute-start | bytes 1105928 | tf_op jit(solution)/shard_map/ppermute | solution.py:27
  11.3 5.8 %collective-permute-done = f32[6,3,40,128]{3,2,1,0:T(8,128)S(1)} collective-permute-done((f32[6,3,40,128]{3,2,1,0:T(8,128)S(1)}, f32[6,3,40,128]{3,2,1,0:T(8,128)S(1)}, u32[]{:S(2)}, u32[]{:S(2)}) %collective-permute-start) | collective-permute-done | bytes 368672 | tf_op jit(solution)/shard_map/ppermute | solution.py:27
  17.1 2.0 %collective-permute-done.1 = f32[6,3,40,128]{3,2,1,0:T(8,128)S(1)} collective-permute-done((f32[6,3,40,128]{3,2,1,0:T(8,128)S(1)}, f32[6,3,40,128]{3,2,1,0:T(8,128)S(1)}, u32[]{:S(2)}, u32[]{:S(2)}) %collective-permute-start.1) | collective-permute-done | bytes 368672 | tf_op jit(solution)/shard_map/ppermute | solution.py:28
  19.5 1.6 %collective-permute-start.3 = (f32[6,10,3,128]{3,2,1,0:T(4,128)S(1)}, f32[6,10,3,128]{3,2,1,0:T(4,128)S(1)}, u32[]{:S(2)}, u32[]{:S(2)}) collective-permute-start(f32[6,10,3,128]{3,2,1,0:T(4,128)S(1)} %get-tuple-element.56), channel_id=1, source_target_pairs={{0,1},{1,2},{2,3},{3,4},{4,5},{5,6},{6,7},{7,8},{8,9},{9,10},{10,1... | collective-permute-start | bytes 276488 | tf_op jit(solution)/shard_map/ppermute | solution.py:27
  21.0 6.3 %collective-permute-start.4 = (f32[6,10,3,128]{3,2,1,0:T(4,128)S(1)}, f32[6,10,3,128]{3,2,1,0:T(4,128)S(1)}, u32[]{:S(2)}, u32[]{:S(2)}) collective-permute-start(f32[6,10,3,128]{3,2,1,0:T(4,128)S(1)} %get-tuple-element.57), channel_id=1, source_target_pairs={{1,0},{2,1},{3,2},{4,3},{5,4},{6,5},{7,6},{8,7},{9,8},{10,9},{11,1... | collective-permute-start | bytes 276488 | tf_op jit(solution)/shard_map/ppermute | solution.py:28
  27.7 2.4 %fusion.7 = f32[5,5,40,128]{3,2,1,0:T(8,128)S(1)} fusion(f32[5,10,40,128]{3,2,1,0:T(8,128)S(1)} %multiply_dynamic-update-slice_fusion.4, f32[5,10,40,128]{3,2,1,0:T(8,128)S(1)} %get-tuple-element.49, f32[5,10,40,128]{3,2,1,0:T(8,128)S(1)} %get-tuple-element.48, pred[5,40,128]{2,1,0:T(8,128)(4,1)S(1)} %fusion.53), kind=kLoop, calls=%fused_computation.29 | loop fusion | flops 17536000 | bytes 7705600 | tf_op jit(solution)/shard_map/jit(_where)/select_n | solution.py:113
  30.7 2.8 %fusion.16 = f32[5,4,41,128]{3,2,1,0:T(8,128)S(1)} fusion(f32[5,4,46,128]{3,2,1,0:T(8,128)S(1)} %multiply_dynamic-update-slice_fusion.12, f32[5,4,46,128]{3,2,1,0:T(8,128)S(1)} %get-tuple-element.51, f32[5,4,46,128]{3,2,1,0:T(8,128)S(1)} %get-tuple-element.50, pred[4,41,128]{2,1,0:T(8,128)(4,1)S(1)} %fusion.56), kind=kLoop, calls=%fused_computation.52 | loop fusion | flops 14379520 | bytes 6318592 | tf_op jit(solution)/shard_map/jit(_where)/select_n | solution.py:113
  35.7 1.9 %copy.31 = f32[4,16,5,40]{3,2,1,0:T(8,128)} copy(f32[4,16,5,40]{1,3,0,2:T(8,128)} %slice_bitcast_fusion.1) | data formatting | bytes 102400 | tf_op jit(solution)/shard_map/transpose | solution.py:254
  38.8 21.1 %shard_map.82 = f32[64,256]{1,0:T(8,128)S(1)} custom-call(f32[64,256]{1,0:T(8,128)S(1)} %pad.7.lines, f32[80,64]{1,0:T(8,128)S(1)} %copy-done.2, f32[64,80]{1,0:T(8,128)S(1)} %copy-done.3, f32[4,40,256]{2,1,0:T(8,128)S(1)} %copy-done.1, f32[16,4,40,256]{3,2,1,0:T(8,128)S(1)} %copy-done), custom_call_target="tpu_custom_call" | custom-call | tf_op jit(solution)/shard_map/pallas_call | solution.py:258
  63.2 1.9 %copy.32 = f32[5,4,40,16]{3,2,1,0:T(8,128)} copy(f32[5,4,40,16]{2,0,3,1:T(8,128)} %copy-done.15) | data formatting | bytes 102400 | tf_op jit(solution)/shard_map/transpose | solution.py:279
  65.1 1.5 %multiply_add_fusion = (f32[1,4,40,128]{3,2,1,0:T(8,128)S(1)}, f32[1,4,40,128]{3,2,1,0:T(8,128)S(1)}, f32[1,4,40,128]{3,2,1,0:T(8,128)S(1)}, f32[1,4,40,128]{3,2,1,0:T(8,128)S(1)}, f32[1,4,40,128]{3,2,1,0:T(8,128)S(1)}) fusion(f32[5,4,40,112]{3,2,1,0:T(8,128)} %slice.924, f32[5,4,40,16]{3,2,1,0:T(8,128)} %copy.32), kind=kLoop, calls=%fused_computation.228 | loop fusion | flops 348160 | bytes 819200 | tf_op jit(solution)/shard_map/add | solution.py:132
  71.8 4.8 %collective-permute-start.5 = (f32[6,3,40,128]{3,2,1,0:T(8,128)}, f32[6,3,40,128]{3,2,1,0:T(8,128)}, u32[]{:S(2)}, u32[]{:S(2)}) collective-permute-start(f32[6,3,40,128]{3,2,1,0:T(8,128)} %get-tuple-element.62), channel_id=1, source_target_pairs={{0,64},{64,128},{128,192},{192,0},{1,65},{65,129},{129,193},{193,1... | collective-permute-start | bytes 1105928 | tf_op jit(solution)/shard_map/ppermute | solution.py:27
  79.5 1.7 %copy.36 = f32[5,4,40,1]{3,2,1,0:T(8,128)} copy(f32[5,4,40,1]{2,1,3,0:T(4,128)} %constant_dynamic-update-slice_fusion.15) | data formatting | bytes 6400 | tf_op jit(solution)/shard_map/stack | solution.py:58
  81.2 3.2 %collective-permute-done.5 = f32[6,3,40,128]{3,2,1,0:T(8,128)} collective-permute-done((f32[6,3,40,128]{3,2,1,0:T(8,128)}, f32[6,3,40,128]{3,2,1,0:T(8,128)}, u32[]{:S(2)}, u32[]{:S(2)}) %collective-permute-start.5) | collective-permute-done | bytes 368672 | tf_op jit(solution)/shard_map/ppermute | solution.py:27
  87.2 1.4 %pad_maximum_fusion.2 = (f32[6,10,40,128]{3,2,1,0:T(8,128)S(1)}, f32[6,10,40,128]{3,2,1,0:T(8,128)S(1)}) fusion(f32[6,3,40,128]{3,2,1,0:T(8,128)S(1)} %broadcast_select_fusion, f32[6,3,40,128]{3,2,1,0:T(8,128)S(1)} %broadcast_select_fusion.1, f32[1,4,40,128]{3,2,1,0:T(8,128)S(1)} %get-tuple-element.75, f32[5,4,40,112]{3,2,1,0:T(8,128)S(1)} %copy-done.6, ...), kind=kLoop, calls=%fused_computation.4 | loop fusion | flops 1843200 | bytes 4423680 | tf_op jit(solution)/shard_map/concatenate | solution.py:298
  88.6 1.3 collective-permute-start.8
  89.9 4.5 %collective-permute-start.9 = (f32[6,10,3,128]{3,2,1,0:T(4,128)S(1)}, f32[6,10,3,128]{3,2,1,0:T(4,128)S(1)}, u32[]{:S(2)}, u32[]{:S(2)}) collective-permute-start(f32[6,10,3,128]{3,2,1,0:T(4,128)S(1)} %get-tuple-element.55), channel_id=1, source_target_pairs={{1,0},{2,1},{3,2},{4,3},{5,4},{6,5},{7,6},{8,7},{9,8},{10,9},{11,1... | collective-permute-start | bytes 276488 | tf_op jit(solution)/shard_map/ppermute | solution.py:28
  94.8 2.4 %fusion.3 = f32[5,5,40,128]{3,2,1,0:T(8,128)S(1)} fusion(f32[5,10,40,128]{3,2,1,0:T(8,128)S(1)} %multiply_dynamic-update-slice_fusion, f32[5,10,40,128]{3,2,1,0:T(8,128)S(1)} %get-tuple-element.47, f32[5,10,40,128]{3,2,1,0:T(8,128)S(1)} %get-tuple-element.46, pred[5,40,128]{2,1,0:T(8,128)(4,1)S(1)} %fusion.54), kind=kLoop, calls=%fused_computation.21 | loop fusion | flops 17536000 | bytes 7705600 | tf_op jit(solution)/shard_map/jit(_where)/select_n | solution.py:113
  99.2 2.8 %fusion.11 = f32[5,4,41,128]{3,2,1,0:T(8,128)S(1)} fusion(f32[5,4,46,128]{3,2,1,0:T(8,128)S(1)} %multiply_dynamic-update-slice_fusion.8, f32[5,4,46,128]{3,2,1,0:T(8,128)S(1)} %subtract_multiply_fusion.2, f32[5,4,46,128]{3,2,1,0:T(8,128)S(1)} %get-tuple-element.14, pred[4,41,128]{2,1,0:T(8,128)(4,1)S(1)} %fusion.55), kind=kLoop, calls=%fused_computation.37 | loop fusion | flops 14379520 | bytes 6318592 | tf_op jit(solution)/shard_map/jit(_where)/select_n | solution.py:113
  104.3 1.9 %copy.37 = f32[4,16,5,40]{3,2,1,0:T(8,128)} copy(f32[4,16,5,40]{1,3,0,2:T(8,128)} %slice_bitcast_fusion) | data formatting | bytes 102400 | tf_op jit(solution)/shard_map/transpose | solution.py:254
  107.3 19.6 %shard_map.83 = f32[64,256]{1,0:T(8,128)S(1)} custom-call(f32[64,256]{1,0:T(8,128)S(1)} %pad.8.lines, f32[80,64]{1,0:T(8,128)S(1)} %copy-done.2, f32[64,80]{1,0:T(8,128)S(1)} %copy-done.3, f32[4,40,256]{2,1,0:T(8,128)S(1)} %copy-done.1, f32[16,4,40,256]{3,2,1,0:T(8,128)S(1)} %copy-done), custom_call_target="tpu_custom_call" | custom-call | tf_op jit(solution)/shard_map/pallas_call | solution.py:258
  (151 shorter events, 29.4 us)
Async XLA Ops:
  0.0 9.7 %copy-start.4 = (f32[5,4,40,128]{3,2,1,0:T(8,128)S(1)}, f32[5,4,40,128]{3,2,1,0:T(8,128)}, u32[]{:S(2)}) copy-start(f32[5,4,40,128]{3,2,1,0:T(8,128)} %param.8) | copy-start | bytes 1228804
  2.0 8.2 %collective-permute-start.2 = (f32[5,4,40]{2,1,0:T(4,128)S(1)}, f32[5,4,40]{2,1,0:T(4,128)S(1)}, u32[]{:S(2)}, u32[]{:S(2)}) collective-permute-start(f32[5,4,40]{2,1,0:T(4,128)S(1)} %bitcast_multiply_fusion), channel_id=1, source_target_pairs={{0,32},{1,33},{2,34},{3,35},{4,36},{5,37},{6,38},{7,39},{8,40},{9,... | collective-permute-start | bytes 9608 | tf_op jit(solution)/shard_map/ppermute | solution.py:35
  6.2 10.8 %collective-permute-start = (f32[6,3,40,128]{3,2,1,0:T(8,128)S(1)}, f32[6,3,40,128]{3,2,1,0:T(8,128)S(1)}, u32[]{:S(2)}, u32[]{:S(2)}) collective-permute-start(f32[6,3,40,128]{3,2,1,0:T(8,128)S(1)} %get-tuple-element.68), channel_id=1, source_target_pairs={{0,64},{64,128},{128,192},{192,0},{1,65},{65,129},{129,193},{193,1... | collective-permute-start | bytes 1105928 | tf_op jit(solution)/shard_map/ppermute | solution.py:27
  9.7 9.4 %collective-permute-start.1 = (f32[6,3,40,128]{3,2,1,0:T(8,128)S(1)}, f32[6,3,40,128]{3,2,1,0:T(8,128)S(1)}, u32[]{:S(2)}, u32[]{:S(2)}) collective-permute-start(f32[6,3,40,128]{3,2,1,0:T(8,128)S(1)} %get-tuple-element.69), channel_id=1, source_target_pairs={{64,0},{128,64},{192,128},{0,192},{65,1},{129,65},{193,129},{1,193... | collective-permute-start | bytes 1105928 | tf_op jit(solution)/shard_map/ppermute | solution.py:28
  9.9 23.6 %copy-start.18 = (f32[128]{0:T(128)}, f32[128]{0:T(128)S(1)}, u32[]{:S(2)}) copy-start(f32[128]{0:T(128)S(1)} %get-tuple-element.81) | copy-start | bytes 1540
  9.9 23.6 %copy-start.20 = (f32[128]{0:T(128)}, f32[128]{0:T(128)S(1)}, u32[]{:S(2)}) copy-start(f32[128]{0:T(128)S(1)} %get-tuple-element.82) | copy-start | bytes 1540
  10.0 23.5 %copy-start.22 = (f32[5]{0:T(128)}, f32[5]{0:T(128)S(1)}, u32[]{:S(2)}) copy-start(f32[5]{0:T(128)S(1)} %pad.62.clone) | copy-start | bytes 64
  10.0 23.5 %copy-start.24 = (f32[5]{0:T(128)}, f32[5]{0:T(128)S(1)}, u32[]{:S(2)}) copy-start(f32[5]{0:T(128)S(1)} %pad.59.clone) | copy-start | bytes 64
  19.5 10.7 %collective-permute-start.3 = (f32[6,10,3,128]{3,2,1,0:T(4,128)S(1)}, f32[6,10,3,128]{3,2,1,0:T(4,128)S(1)}, u32[]{:S(2)}, u32[]{:S(2)}) collective-permute-start(f32[6,10,3,128]{3,2,1,0:T(4,128)S(1)} %get-tuple-element.56), channel_id=1, source_target_pairs={{0,1},{1,2},{2,3},{3,4},{4,5},{5,6},{6,7},{7,8},{8,9},{9,10},{10,1... | collective-permute-start | bytes 276488 | tf_op jit(solution)/shard_map/ppermute | solution.py:27
  21.0 9.2 %collective-permute-start.4 = (f32[6,10,3,128]{3,2,1,0:T(4,128)S(1)}, f32[6,10,3,128]{3,2,1,0:T(4,128)S(1)}, u32[]{:S(2)}, u32[]{:S(2)}) collective-permute-start(f32[6,10,3,128]{3,2,1,0:T(4,128)S(1)} %get-tuple-element.57), channel_id=1, source_target_pairs={{1,0},{2,1},{3,2},{4,3},{5,4},{6,5},{7,6},{8,7},{9,8},{10,9},{11,1... | collective-permute-start | bytes 276488 | tf_op jit(solution)/shard_map/ppermute | solution.py:28
  33.5 5.2 %copy-start.1 = (f32[4,40,256]{2,1,0:T(8,128)S(1)}, f32[4,40,256]{2,1,0:T(8,128)}, u32[]{:S(2)}) copy-start(f32[4,40,256]{2,1,0:T(8,128)} %constant.121.clone.twiddle) | copy-start | bytes 491524
  34.0 4.8 %copy-start = (f32[16,4,40,256]{3,2,1,0:T(8,128)S(1)}, f32[16,4,40,256]{3,2,1,0:T(8,128)}, u32[]{:S(2)}) copy-start(f32[16,4,40,256]{3,2,1,0:T(8,128)} %constant.122.clone.band) | copy-start | bytes 7864324
  34.0 4.8 %copy-start.2 = (f32[80,64]{1,0:T(8,128)S(1)}, f32[80,64]{1,0:T(8,128)}, u32[]{:S(2)}) copy-start(f32[80,64]{1,0:T(8,128)} %constant.119.clone.fwd) | copy-start | bytes 61444
  34.0 4.8 %copy-start.3 = (f32[64,80]{1,0:T(8,128)S(1)}, f32[64,80]{1,0:T(8,128)}, u32[]{:S(2)}) copy-start(f32[64,80]{1,0:T(8,128)} %constant.120.clone.inv) | copy-start | bytes 61444
  38.8 23.7 %copy-start.26 = (f32[5]{0:T(128)S(1)}, f32[5]{0:T(128)}, u32[]{:S(2)}) copy-start(f32[5]{0:T(128)} %constant.123.clone) | copy-start | bytes 64
  68.4 8.2 %collective-permute-start.7 = (f32[5,4,40]{2,0,1:T(8,128)S(1)}, f32[5,4,40]{2,0,1:T(8,128)S(1)}, u32[]{:S(2)}, u32[]{:S(2)}) collective-permute-start(f32[5,4,40]{2,0,1:T(8,128)S(1)} %copy-done.17), channel_id=1, source_target_pairs={{0,32},{1,33},{2,34},{3,35},{4,36},{5,37},{6,38},{7,39},{8,40},{9,... | collective-permute-start | bytes 9608 | tf_op jit(solution)/shard_map/ppermute | solution.py:35
  71.8 12.6 %collective-permute-start.5 = (f32[6,3,40,128]{3,2,1,0:T(8,128)}, f32[6,3,40,128]{3,2,1,0:T(8,128)}, u32[]{:S(2)}, u32[]{:S(2)}) collective-permute-start(f32[6,3,40,128]{3,2,1,0:T(8,128)} %get-tuple-element.62), channel_id=1, source_target_pairs={{0,64},{64,128},{128,192},{192,0},{1,65},{65,129},{129,193},{193,1... | collective-permute-start | bytes 1105928 | tf_op jit(solution)/shard_map/ppermute | solution.py:27
  76.6 9.5 %collective-permute-start.6 = (f32[6,3,40,128]{3,2,1,0:T(8,128)}, f32[6,3,40,128]{3,2,1,0:T(8,128)}, u32[]{:S(2)}, u32[]{:S(2)}) collective-permute-start(f32[6,3,40,128]{3,2,1,0:T(8,128)} %get-tuple-element.63), channel_id=1, source_target_pairs={{64,0},{128,64},{192,128},{0,192},{65,1},{129,65},{193,129},{1,193... | collective-permute-start | bytes 1105928 | tf_op jit(solution)/shard_map/ppermute | solution.py:28
  81.2 5.9 %copy-start.6 = (f32[5,4,40,112]{3,2,1,0:T(8,128)S(1)}, f32[5,4,40,112]{3,2,1,0:T(8,128)}, u32[]{:S(2)}) copy-start(f32[5,4,40,112]{3,2,1,0:T(8,128)} %slice.924) | copy-start | bytes 1075204
  81.2 5.9 %copy-start.8 = (f32[5,4,40,16]{3,2,1,0:T(8,128)S(1)}, f32[5,4,40,16]{3,2,1,0:T(8,128)}, u32[]{:S(2)}) copy-start(f32[5,4,40,16]{3,2,1,0:T(8,128)} %copy.32) | copy-start | bytes 153604
  88.6 9.6 %collective-permute-start.8 = (f32[6,10,3,128]{3,2,1,0:T(4,128)S(1)}, f32[6,10,3,128]{3,2,1,0:T(4,128)S(1)}, u32[]{:S(2)}, u32[]{:S(2)}) collective-permute-start(f32[6,10,3,128]{3,2,1,0:T(4,128)S(1)} %get-tuple-element.54), channel_id=1, source_target_pairs={{0,1},{1,2},{2,3},{3,4},{4,5},{5,6},{6,7},{7,8},{8,9},{9,10},{10,1... | collective-permute-start | bytes 276488 | tf_op jit(solution)/shard_map/ppermute | solution.py:27
  89.9 8.3 %collective-permute-start.9 = (f32[6,10,3,128]{3,2,1,0:T(4,128)S(1)}, f32[6,10,3,128]{3,2,1,0:T(4,128)S(1)}, u32[]{:S(2)}, u32[]{:S(2)}) collective-permute-start(f32[6,10,3,128]{3,2,1,0:T(4,128)S(1)} %get-tuple-element.55), channel_id=1, source_target_pairs={{1,0},{2,1},{3,2},{4,3},{5,4},{6,5},{7,6},{8,7},{9,8},{10,9},{11,1... | collective-permute-start | bytes 276488 | tf_op jit(solution)/shard_map/ppermute | solution.py:28
  99.1 2.9 %copy-start.10 = (f32[5,4,40,128]{3,2,1,0:T(8,128)S(1)}, f32[5,4,40,128]{3,2,1,0:T(8,128)}, u32[]{:S(2)}) copy-start(f32[5,4,40,128]{3,2,1,0:T(8,128)} %copy-done.9) | copy-start | bytes 1228804
  99.1 2.9 %copy-start.11 = (f32[5,4,40,1]{3,2,1,0:T(8,128)S(1)}, f32[5,4,40,1]{3,2,1,0:T(8,128)}, u32[]{:S(2)}) copy-start(f32[5,4,40,1]{3,2,1,0:T(8,128)} %slice.961) | copy-start | bytes 9604
  (13 other events, 27.1 us)
where the time goes:
time: 130 us; the launch traced here: 129 us
  Pallas kernels  40.7 us (31%)
  other arithmetic  27.4 us (21%)
  starting transfers between devices  24.9 us (19%)
  local copies, waits for them, and re-layouts  22.5 us (17%)
  waiting for transfers between devices  12.6 us (10%)
    pallas_call x2, Pallas kernels, cycle_filter(): pl.pallas_call(filter_kernel, out_shape=jax.ShapeDtypeStruct((64, 256), j...  40.7 us
    ppermute x4, starting transfers between devices, with_halo(): before = lax.ppermute(last, axis, up)  11.1 us
    ppermute x4, starting transfers between devices, with_halo(): after = lax.ppermute(leading, axis, down)  10.8 us
    select_n x4, other arithmetic, face_flux(): return jnp.where(switch[None] > 0.5, plus_face + minus_face, central)  10.4 us
    ppermute x4, waiting for transfers between devices, with_halo(): before = lax.ppermute(last, axis, up)  9.86 us
    transpose x4, local copies, waits for them, and re-layouts, cycle_filter(): lines = jnp.transpose(cycles, (1, 3, 0, 2)).reshape(64, 200)  5.46 us
    unnamed x30, other arithmetic  3.63 us
    unnamed x55, local copies, waits for them, and re-layouts  3.36 us
  transfers between devices with their start and end apart: 10, of which 5 were waited for; matrix products, arithmetic and copies ran while one was open for 13% of the time, Pallas kernels for 0%

commit v1 on v0

v1 whole, which is shorter than its diff:
```python
import math

import jax
import jax.numpy as jnp
import numpy as np
from jax import lax
from jax.experimental import pallas as pl
from jax.experimental.pallas import tpu as pltpu
from jax.sharding import PartitionSpec as P

NRING = 16
MESH = pl.DeviceIdType.MESH

split_speed = 3.0
small_eps = 1e-06
time_step = 0.004


def filter_tables():
    d, k1 = np.arange(64), np.arange(33)
    angle = 2 * np.pi * np.outer(k1, d) / 64
    fwd = np.zeros((80, 64))
    fwd[:33], fwd[40:73] = np.cos(angle), -np.sin(angle)
    inv = np.zeros((64, 80))
    inv[:, :33], inv[:, 40:73] = np.cos(angle.T), -np.sin(angle.T)
    twiddle = np.zeros((4, 40, 256))
    m_in, m_out = np.arange(40), np.arange(-3, 43)
    scale = np.where((k1 == 0) | (k1 == 32), 1.0, 2.0)[:, None] / 2560
    for v in range(5):
        angle = 2 * np.pi * np.outer(k1, m_in) / 2560
        twiddle[0, :33, v * 40 : v * 40 + 40] = np.cos(angle)
        twiddle[1, :33, v * 40 : v * 40 + 40] = -np.sin(angle)
        angle = 2 * np.pi * np.outer(k1, m_out) / 2560
        twiddle[2, :33, v * 48 : v * 48 + 46] = np.cos(angle) * scale
        twiddle[3, :33, v * 48 : v * 48 + 46] = np.sin(angle) * scale
    band = np.zeros((16, 4, 40, 256))
    delta = m_out[None, :] - m_in[:, None]
    for j in range(16):
        if j % 2:
            q = (j + 1) // 2
            modes, extra = np.arange(-q, q), -q
        else:
            q = j // 2
            modes, extra = np.arange(-q, q + 1), q
        kept = sum(np.exp(2j * np.pi * k * delta / 40) for k in modes)
        twin = np.exp(2j * np.pi * extra * delta / 40)
        band[j, 0, :, :46], band[j, 1, :, :46] = kept.real, kept.imag
        band[j, 2, :, :46], band[j, 3, :, :46] = twin.real, twin.imag
    return [a.astype(np.float32) for a in (fwd, inv, twiddle, band)]


def matmul(a, b):
    return jnp.dot(a, b, precision=lax.Precision.HIGHEST, preferred_element_type=jnp.float32)


def inverse(x):
    return pltpu.reciprocal(x, approx=True)


class Rows:
    def __init__(self, cells):
        self.cells = list(cells)

    def _with(self, other, op):
        if isinstance(other, Rows):
            pairs = zip(self.cells, other.cells)
            return Rows([None if a is None or b is None else op(a, b) for a, b in pairs])
        return Rows([None if a is None else op(a, other) for a in self.cells])

    def __add__(self, other):
        return self._with(other, lambda a, b: a + b)

    def __sub__(self, other):
        return self._with(other, lambda a, b: a - b)

    def __mul__(self, other):
        return self._with(other, lambda a, b: a * b)

    def map(self, op):
        return Rows([None if a is None else op(a) for a in self.cells])

    def shifted(self, by):
        n = len(self.cells)
        return Rows([self.cells[k + by] if 0 <= k + by < n else None for k in range(n)])


def at(x, by):
    if isinstance(x, Rows):
        return x.shifted(by)
    n = x.shape[0]
    return pltpu.roll(x, (n - by) % n, 0)


def inverse_of(x):
    return x.map(inverse) if isinstance(x, Rows) else inverse(x)


def indicators(f):
    d = at(f, 1) - f
    s = d - at(d, -1)
    s_next = at(s, 1)
    e = s - s_next
    h = s * 0.5
    q = s * s * (13.0 / 12.0) + small_eps
    mid = d - h
    up = d + h
    down = mid - s
    x = inverse_of(q + up * up)
    y = inverse_of(q + mid * mid)
    z = inverse_of(q + down * down)
    return d, s, s_next, e, x * x, y * y, z * z


def faces(flux, state, switch, choose):
    half = flux * 0.5
    lift = state * (0.5 * split_speed)
    d_p, s_p, sn_p, e_p, x_p, y_p, z_p = indicators(half + lift)
    zn_p = at(z_p, 1)
    top = at(x_p * e_p, -1) * 2.0 + zn_p * e_p * 3.0
    total = at(x_p, -1) + y_p * 6.0 + zn_p * 3.0
    plus = top * inverse_of(total)
    d_m, s_m, sn_m, e_m, x_m, y_m, z_m = indicators(half - lift)
    zn_m = at(z_m, 1)
    top = at(zn_m * e_m, 1) * 2.0 + x_m * e_m * 3.0
    total = at(zn_m, 1) + at(y_m, 1) * 6.0 + x_m * 3.0
    minus = top * inverse_of(total)
    middle = flux + (d_p + d_m) * 0.5
    own = s_p + sn_m
    weno = (plus - minus - own) * (1.0 / 6.0)
    central = (own + s_m + sn_p) * (-1.0 / 12.0)
    return middle + choose(switch, weno, central)


def pick(switch, a, b):
    if isinstance(a, Rows):
        triples = zip(switch.cells, a.cells, b.cells)
        return Rows([None if s is None or p is None or q is None else jnp.where(s, p, q) for s, p, q in triples])
    return jnp.where(switch, a, b)


def largest(a, b):
    if isinstance(a, Rows):
        return a._with(b, jnp.maximum)
    return jnp.maximum(a, b)


def window(flags):
    pair = largest(flags, at(flags, 1))
    four = largest(pair, at(pair, 2))
    six = at(largest(four, at(pair, 4)), -2)
    return six.map(lambda a: a > 0.5) if isinstance(six, Rows) else six > 0.5


def fluxes(u, q, p, component):
    parts = [u[1 + component], u[1] * q, u[2] * q, u[3] * q, (u[4] + p) * q]
    parts[1 + component] = parts[1 + component] + p
    return parts


def pressure(u, inv_rho):
    return (u[4] - (u[1] * u[1] + u[2] * u[2] + u[3] * u[3]) * inv_rho * 0.5) * 0.4


def lanes(shape):
    return lax.broadcasted_iota(jnp.int32, shape, len(shape) - 1)


def radius(rows):
    return lanes((rows, 128)).astype(jnp.float32) + 0.5


def azimuthal(padded, flags, section, rate):
    scale = -1.0 / (radius(40) * (2.0 * math.pi / 2560))

    def row(r, carry):
        u = [padded[v, r] for v in range(5)]
        inv_rho = inverse(u[0])
        q = u[3] * inv_rho
        f = fluxes(u, q, pressure(u, inv_rho), 2)
        switch = window(flags[section, r])
        for v in range(5):
            face = faces(f[v], u[v], switch, pick)
            rate[v, r] = (at(face, 3)[:40] - at(face, 2)[:40]) * scale
        return carry

    lax.fori_loop(0, 4, row, 0)


def finish(own, low, high, flags, flags_low, flags_high, section, ghost, rate, combine):
    inv_r = 1.0 / radius(8)
    lane = lanes((8, 128))
    signs = [1.0, 1.0, -1.0, -1.0, 1.0]

    def chunk(c, carry):
        at8 = pl.ds(pl.multiple_of(c * 8, 8), 8)
        u = [
            Rows(
                [low[v, k, at8, :] for k in range(3)]
                + [own[v, k, at8, :] for k in range(4)]
                + [high[v, k, at8, :] for k in range(3)]
            )
            for v in range(5)
        ]
        marks = Rows(
            [flags_low[section, k, at8, :] for k in range(3)]
            + [flags[section, k, at8, :] for k in range(4)]
            + [flags_high[section, k, at8, :] for k in range(3)]
        ).map(lambda a: a.astype(jnp.float32))
        switch = window(marks)
        inv_rho = u[0].map(inverse)
        p = pressure(u, inv_rho)
        f = fluxes(u, u[1] * inv_rho, p, 0)
        columns = ghost[at8, :]
        radial, source = [], []
        for r in range(4):
            here = [u[v].cells[3 + r] for v in range(5)]
            there = [pltpu.roll(columns, (128 - (v * 4 + r)) % 128, 1) * signs[v] for v in range(5)]
            there[0] = jnp.where(lane == 0, there[0], 1.0)
            there_inv = inverse(there[0])
            g_ghost = fluxes(there, there[2] * there_inv, pressure(there, there_inv), 1)
            inv_here, p_here = inv_rho.cells[3 + r], p.cells[3 + r]
            g = fluxes(here, here[2] * inv_here, p_here, 1)
            swirl = here[3] * inv_here
            extra = [None, None, here[3] * swirl + p_here, -here[2] * swirl, None]
            terms = []
            for v in range(5):
                before = jnp.where(lane == 0, g_ghost[v], pltpu.roll(g[v], 1, 1))
                after = jnp.where(lane == 127, g[v], pltpu.roll(g[v], 127, 1))
                away = g[v] if extra[v] is None else g[v] - extra[v]
                terms.append((after - before) * 0.5 + away * inv_r)
            radial.append(terms)
        for v in range(5):
            face = faces(f[v], u[v], switch, pick).cells
            for r in range(4):
                slope = rate[v, r, at8, :] - (face[3 + r] - face[2 + r]) - radial[r][v]
                combine(v, r, at8, u[v].cells[3 + r], slope)
        return carry

    lax.fori_loop(0, 5, chunk, 0)


def ghost_columns(field, staging):
    lane = lanes((40, 128))
    packed = jnp.zeros((40, 128), jnp.float32)
    for v in range(5):
        for r in range(4):
            k = v * 4 + r
            value = field[v, r]
            packed = jnp.where(lane == k, pltpu.roll(value, k, 1) if k else value, packed)
    staging[...] = packed


def to_lines(field, send):
    for r in range(4):
        stack = [field[v, r] for v in range(5)] + [jnp.zeros((56, 128), jnp.float32)]
        turned = jnp.transpose(jnp.concatenate(stack, axis=0))[:16]
        send[16 * r : 16 * r + 16, 0, :] = turned[:, :128]
        send[16 * r : 16 * r + 16, 1, :] = turned[:, 128:]


def from_lines(ret, first):
    lines = jnp.concatenate([ret[first : first + 16, 0, :], ret[first : first + 16, 1, :]], axis=1)
    lines = jnp.concatenate([lines, jnp.zeros((112, 256), jnp.float32)], axis=0)
    turned = jnp.transpose(lines)
    return [turned[48 * v : 48 * v + 48] for v in range(5)]


def spread(send, recv, me, send_sem, recv_sem):
    def one(i, carry):
        to = lax.rem(me + i, 64)
        pltpu.make_async_remote_copy(
            src_ref=send.at[to],
            dst_ref=recv.at[me],
            send_sem=send_sem,
            recv_sem=recv_sem,
            device_id={"az": to},
            device_id_type=MESH,
        ).start()
        return carry

    lax.fori_loop(1, 64, one, 0)
    recv[pl.ds(me, 1)] = send[pl.ds(me, 1)]


def arrived(buffer, sem):
    rows = buffer.at[pl.ds(0, 63)]
    pltpu.make_async_copy(rows, rows, sem).wait()


def build_mix(mine, mix):
    mix[...] = jnp.zeros_like(mix)
    for part in range(2):
        re, im = mine[2 * part], mine[2 * part + 1]
        for v in range(5):
            c = pltpu.roll(re, 48 * v, 1) if v else re
            s = pltpu.roll(im, 48 * v, 1) if v else im
            row = 512 * part + 40 * v
            mix[row : row + 40, :256] = c
            mix[row : row + 40, 256:] = s
            mix[row + 256 : row + 296, :256] = -s
            mix[row + 256 : row + 296, 256:] = c


def project(recv, back, me, fwd, inv, twiddle, mix):
    x = jnp.concatenate([recv[:, 0, :], recv[:, 1, :]], axis=1)
    a = matmul(fwd[...], x)
    re, im = a[:40], a[40:]
    re, im = re * twiddle[0] - im * twiddle[1], re * twiddle[1] + im * twiddle[0]
    special = jnp.where(lax.rem(me, 2) == 1, 0, 32)
    own = (lax.broadcasted_iota(jnp.int32, (40, 256), 0) == special).astype(jnp.float32)
    z = matmul(jnp.concatenate([re, im, re * own, im * own], axis=1), mix[...])
    re, im = z[:, :256], z[:, 256:]
    re, im = re * twiddle[2] - im * twiddle[3], re * twiddle[3] + im * twiddle[2]
    y = matmul(inv[...], jnp.concatenate([re, im], axis=0))
    back[:, 0, :] = y[:, :128]
    back[:, 1, :] = y[:, 128:]


def kernel(
    state, flags, fwd, inv, twiddle, band, out,
    mine, mix, padded, padded_flags, rate, first, second,
    az_out, az_in, azf_out, azf_in, low, high, flow, fhigh, ghost_out, ghost_in, near_low, near_high,
    send, recv, back, ret,
    sem, az_sem, azf_sem, ax_sem, axf_sem, ghost_sem, near_sem, go_sem, come_sem,
):
    me, row = lax.axis_index("az"), lax.axis_index("ax")
    right, left = lax.rem(me + 1, 64), lax.rem(me + 63, 64)
    load = pltpu.make_async_copy(band.at[lax.rem(me, 16)], mine, sem)
    load.start()
    barrier = pltpu.get_barrier_semaphore()

    def greet(i, carry):
        peer = lax.rem(me + i, 64)
        pl.semaphore_signal(barrier, inc=1, device_id={"az": peer}, device_id_type=MESH)
        return carry

    lax.fori_loop(1, 64, greet, 0)
    for by in (1, 3):
        peer = lax.rem(row + by, 4)
        pl.semaphore_signal(barrier, inc=1, device_id={"ax": peer}, device_id_type=MESH)

    def copy(src, dst, sems, k, **place):
        return pltpu.make_async_remote_copy(
            src_ref=src,
            dst_ref=dst,
            send_sem=sems.at[0, k],
            recv_sem=sems.at[1, k],
            device_id=place,
            device_id_type=MESH,
        )

    def az_copies(section):
        return [
            copy(az_out.at[0], az_in.at[section, 0], az_sem.at[section], 0, az=right),
            copy(az_out.at[1], az_in.at[section, 1], az_sem.at[section], 1, az=left),
        ]

    def ax_copies(field, to_low, to_high, sems):
        up = copy(field.at[:, pl.ds(1, 3)], to_low, sems, 0, ax=lax.rem(row + 1, 4))
        down = copy(field.at[:, pl.ds(0, 3)], to_high, sems, 1, ax=lax.rem(row + 3, 4))
        return up, down

    def stage(field, staging, fields):
        for f in range(fields):
            for r in range(4):
                staging[0, f * 4 + r, 0:3] = field[f, r, 37:40]
                staging[1, f * 4 + r, 0:3] = field[f, r, 0:3]

    def when_up(action):
        pl.when(row < 3)(action)

    def when_down(action):
        pl.when(row > 0)(action)

    def start_ax(pair):
        when_up(pair[0].start)
        when_down(pair[1].start)

    def sent_ax(pair):
        when_up(pair[0].wait_send)
        when_down(pair[1].wait_send)

    def came_ax(pair):
        when_down(pair[0].wait_recv)
        when_up(pair[1].wait_recv)

    stage(state, az_out, 5)
    stage(flags, azf_out, 2)
    ghost_columns(state, ghost_out)
    az = az_copies(0)
    azf = [
        copy(azf_out.at[0], azf_in.at[0], azf_sem, 0, az=right),
        copy(azf_out.at[1], azf_in.at[1], azf_sem, 1, az=left),
    ]
    opposite = lax.rem(me + 32, 64)
    ghost = copy(ghost_out, ghost_in.at[0], ghost_sem.at[0], 0, az=opposite)
    ax = ax_copies(state, low.at[0], high.at[0], ax_sem.at[0])
    axf = ax_copies(flags, flow, fhigh, axf_sem)
    pl.semaphore_wait(barrier, 65)
    for item in az + azf:
        item.start()
    start_ax(ax)
    start_ax(axf)
    ghost.start()
    load.wait()
    build_mix(mine, mix)
    padded[...] = jnp.zeros_like(padded)
    padded_flags[...] = jnp.zeros_like(padded_flags)
    for v in range(5):
        for r in range(4):
            padded[v, r, 3:43] = state[v, r]
    for s in range(2):
        for r in range(4):
            padded_flags[s, r, 3:43] = flags[s, r].astype(jnp.float32)

    def fill_az(section):
        for v in range(5):
            for r in range(4):
                padded[v, r, 0:3] = az_in[section, 0, v * 4 + r, 0:3]
                padded[v, r, 43:46] = az_in[section, 1, v * 4 + r, 0:3]

    for item in az + azf:
        item.wait_send()
        item.wait_recv()
    fill_az(0)
    for s in range(2):
        for r in range(4):
            padded_flags[s, r, 0:3] = azf_in[0, s * 4 + r, 0:3].astype(jnp.float32)
            padded_flags[s, r, 43:46] = azf_in[1, s * 4 + r, 0:3].astype(jnp.float32)
    azimuthal(padded, padded_flags, 0, rate)
    came_ax(ax)
    came_ax(axf)

    def rims(field, section):
        def low_rim():
            for v in range(5):
                for k in range(3):
                    low[section, v, k] = field[v, 0]

        def high_rim():
            for v in range(5):
                for k in range(3):
                    high[section, v, k] = field[v, 3]

        pl.when(row == 0)(low_rim)
        pl.when(row == 3)(high_rim)

    def flag_low_rim():
        for s in range(2):
            for k in range(3):
                flow[s, k] = flags[s, 0]

    def flag_high_rim():
        for s in range(2):
            for k in range(3):
                fhigh[s, k] = flags[s, 3]

    rims(state, 0)
    pl.when(row == 0)(flag_low_rim)
    pl.when(row == 3)(flag_high_rim)
    ghost.wait_send()
    ghost.wait_recv()

    def combine_first(v, r, rows, here, slope):
        first[v, r, rows, :] = here + slope * time_step

    finish(state, low.at[0], high.at[0], flags, flow, fhigh, 0, ghost_in.at[0], rate, combine_first)
    sent_ax(ax)
    sent_ax(axf)

    to_lines(first, send.at[0])
    spread(send.at[0], recv.at[0], me, go_sem.at[0, 0], go_sem.at[0, 1])
    stage(first, az_out, 5)
    az = az_copies(1)
    for item in az:
        item.start()
    ax = ax_copies(first, low.at[1], high.at[1], ax_sem.at[1])
    start_ax(ax)
    for v in range(5):
        for r in range(4):
            padded[v, r, 3:43] = first[v, r]
    arrived(recv.at[0], go_sem.at[0, 1])
    project(recv.at[0], back.at[0], me, fwd, inv, twiddle, mix)
    spread(back.at[0], ret.at[0], me, come_sem.at[0, 0], come_sem.at[0, 1])
    for item in az:
        item.wait_send()
        item.wait_recv()
    fill_az(1)
    sent_ax(ax)
    came_ax(ax)
    arrived(ret.at[0], come_sem.at[0, 1])

    near = (
        copy(ret.at[0, pl.ds(16, 48)], near_low, near_sem, 0, ax=lax.rem(row + 1, 4)),
        copy(ret.at[0, pl.ds(0, 48)], near_high, near_sem, 1, ax=lax.rem(row + 3, 4)),
    )
    start_ax(near)
    inner48, inner40 = lanes((48, 128)) < NRING, lanes((40, 128)) < NRING
    for r in range(4):
        blocks = from_lines(ret.at[0], 16 * r)
        for v in range(5):
            merged = jnp.where(inner48, blocks[v], padded[v, r])
            padded[v, r] = merged
            first[v, r] = merged[3:43]
    ghost_columns(first, ghost_out)
    ghost = copy(ghost_out, ghost_in.at[1], ghost_sem.at[1], 0, az=opposite)
    ghost.start()
    azimuthal(padded, padded_flags, 1, rate)
    came_ax(near)

    def merge_low():
        for k in range(3):
            blocks = from_lines(near_low, 16 * k)
            for v in range(5):
                low[1, v, k] = jnp.where(inner40, blocks[v][3:43], low[1, v, k])

    def merge_high():
        for k in range(3):
            blocks = from_lines(near_high, 16 * k)
            for v in range(5):
                high[1, v, k] = jnp.where(inner40, blocks[v][3:43], high[1, v, k])

    when_down(merge_low)
    when_up(merge_high)
    rims(first, 1)
    ghost.wait_send()
    ghost.wait_recv()

    def combine_second(v, r, rows, here, slope):
        second[v, r, rows, :] = state[v, r, rows, :] * 0.75 + (here + slope * time_step) * 0.25

    finish(first, low.at[1], high.at[1], flags, flow, fhigh, 1, ghost_in.at[1], rate, combine_second)
    sent_ax(near)

    to_lines(second, send.at[1])
    spread(send.at[1], recv.at[1], me, go_sem.at[1, 0], go_sem.at[1, 1])
    arrived(recv.at[1], go_sem.at[1, 1])
    project(recv.at[1], back.at[1], me, fwd, inv, twiddle, mix)
    spread(back.at[1], ret.at[1], me, come_sem.at[1, 0], come_sem.at[1, 1])
    arrived(ret.at[1], come_sem.at[1, 1])
    for r in range(4):
        blocks = from_lines(ret.at[1], 16 * r)
        for v in range(5):
            out[v, r] = jnp.where(inner40, blocks[v][3:43], second[v, r]) - state[v, r]
    for section in range(2):
        arrived(send.at[section], go_sem.at[section, 0])
        arrived(back.at[section], come_sem.at[section, 0])


def local(state, shock_flags):
    tables = [jnp.asarray(t) for t in filter_tables()]
    vmem = pl.BlockSpec(memory_space=pltpu.VMEM)
    f32, i32 = jnp.float32, jnp.int32
    dma = pltpu.SemaphoreType.DMA
    return pl.pallas_call(
        kernel,
        out_shape=jax.ShapeDtypeStruct(state.shape, f32),
        in_specs=[vmem] * 5 + [pl.BlockSpec(memory_space=pl.ANY)],
        out_specs=vmem,
        scratch_shapes=[
            pltpu.VMEM((4, 40, 256), f32),
            pltpu.VMEM((1024, 512), f32),
            pltpu.VMEM((5, 4, 48, 128), f32),
            pltpu.VMEM((2, 4, 48, 128), f32),
            pltpu.VMEM((5, 4, 40, 128), f32),
            pltpu.VMEM((5, 4, 40, 128), f32),
            pltpu.VMEM((5, 4, 40, 128), f32),
            pltpu.VMEM((2, 20, 4, 128), f32),
            pltpu.VMEM((2, 2, 20, 4, 128), f32),
            pltpu.VMEM((2, 8, 4, 128), i32),
            pltpu.VMEM((2, 8, 4, 128), i32),
            pltpu.VMEM((2, 5, 3, 40, 128), f32),
            pltpu.VMEM((2, 5, 3, 40, 128), f32),
            pltpu.VMEM((2, 3, 40, 128), i32),
            pltpu.VMEM((2, 3, 40, 128), i32),
            pltpu.VMEM((40, 128), f32),
            pltpu.VMEM((2, 40, 128), f32),
            pltpu.VMEM((48, 2, 128), f32),
            pltpu.VMEM((48, 2, 128), f32),
            pltpu.VMEM((2, 64, 2, 128), f32),
            pltpu.VMEM((2, 64, 2, 128), f32),
            pltpu.VMEM((2, 64, 2, 128), f32),
            pltpu.VMEM((2, 64, 2, 128), f32),
            dma,
            dma((2, 2, 2)),
            dma((2, 2)),
            dma((2, 2, 2)),
            dma((2, 2)),
            dma((2, 2, 1)),
            dma((2, 2)),
            dma((2, 2)),
            dma((2, 2)),
        ],
        compiler_params=pltpu.CompilerParams(
            collective_id=0, has_side_effects=True, vmem_limit_bytes=48 * 1024 * 1024
        ),
    )(state, shock_flags, *tables)


def solution(mesh):
    in_specs = (P(None, "ax", "az", None), P(None, "ax", "az", None))
    out_specs = P(None, "ax", "az", None)
    return jax.shard_map(local, mesh=mesh, in_specs=in_specs, out_specs=out_specs, check_vma=False)
```

time: 130 us -> 66.5 us (0.51)
  other arithmetic: 27.4 us -> 0 us
  starting transfers between devices: 24.9 us -> 0 us
  Pallas kernels: 40.7 us -> 59.3 us
  local copies, waits for them, and re-layouts: 22.5 us -> 6.86 us
  waiting for transfers between devices: 12.6 us -> 0 us
    ppermute x10 -> x0, starting transfers between devices: 24.9 us -> none  [the longest x4 11.1 us: with_halo(): before = lax.ppermute(last, axis, up)]
    pallas_call x2 -> x1, Pallas kernels: 40.7 us -> 59.3 us  [local(): pl.pallas_call(kernel, out_shape=jax.ShapeDtypeStruct(state.shape, f32),...]
    ppermute x10 -> x0, waiting for transfers between devices: 12.6 us -> none  [the longest x4 9.86 us: with_halo(): before = lax.ppermute(last, axis, up)]
    select_n x8 -> x0, other arithmetic: 12.5 us -> none  [the longest x4 10.4 us: face_flux(): return jnp.where(switch[None] > 0.5, plus_face + minus_face, central)]
    transpose x8 -> x0, local copies, waits for them, and re-layouts: 8.76 us -> none  [the longest x4 5.46 us: cycle_filter(): lines = jnp.transpose(cycles, (1, 3, 0, 2)).reshape(64, 200)]
    slice x8 -> x0, local copies, waits for them, and re-layouts: 4.01 us -> none  [the longest x2 1.85 us: cycle_filter(): return jnp.concatenate([smooth_cycles, conserved[..., NRING:]], axis=3)]
    unnamed x30 -> x0, other arithmetic: 3.63 us -> none
    unnamed x55 -> x13, local copies, waits for them, and re-layouts: 3.36 us -> 6.86 us
  transfers between devices with their start and end apart: 10 -> 0, of which waited for: 5 -> 0; matrix products, arithmetic and copies ran while one was open for 13% -> 0% of each run, Pallas kernels for 0% -> 0%
where the time goes in v1:
time: 66.5 us; the launch traced here: 66.2 us
  Pallas kernels  59.3 us (89%)
  local copies, waits for them, and re-layouts  6.86 us (10%)
    pallas_call x1, Pallas kernels, local(): pl.pallas_call(kernel, out_shape=jax.ShapeDtypeStruct(state.shape, f32),...  59.3 us
    unnamed x13, local copies, waits for them, and re-layouts  6.86 us

profile of v1, /device:TPU:1, one launch (start us, length us, event | category | flops | bytes accessed | tf_op | source)
XLA Modules:
  0.0 66.2 jit_solution(17464900248188859472)
XLA Ops:
  0.0 0.0 copy-start
  0.0 1.7 %copy-done = f32[16,4,40,256]{3,2,1,0:T(8,128)S(1)} copy-done((f32[16,4,40,256]{3,2,1,0:T(8,128)S(1)}, f32[16,4,40,256]{3,2,1,0:T(8,128)}, u32[]{:S(2)}) %copy-start) | copy-done | bytes 2621464
  1.7 0.0 copy-start.1
  1.7 1.0 %copy-done.1 = f32[5,4,40,128]{3,2,1,0:T(8,128)S(1)} copy-done((f32[5,4,40,128]{3,2,1,0:T(8,128)S(1)}, f32[5,4,40,128]{3,2,1,0:T(8,128)}, u32[]{:S(2)}) %copy-start.1) | copy-done | bytes 409624
  2.7 0.0 copy-start.2
  2.7 0.9 %copy-done.2 = s32[2,4,40,128]{3,2,1,0:T(8,128)S(1)} copy-done((s32[2,4,40,128]{3,2,1,0:T(8,128)S(1)}, s32[2,4,40,128]{3,2,1,0:T(8,128)}, u32[]{:S(2)}) %copy-start.2) | copy-done | bytes 163864
  3.7 0.0 copy-start.3
  3.7 0.9 %copy-done.3 = f32[4,40,256]{2,1,0:T(8,128)S(1)} copy-done((f32[4,40,256]{2,1,0:T(8,128)S(1)}, f32[4,40,256]{2,1,0:T(8,128)}, u32[]{:S(2)}) %copy-start.3) | copy-done | bytes 163864
  4.6 0.0 copy-start.4
  4.6 0.8 %copy-done.4 = f32[80,64]{1,0:T(8,128)S(1)} copy-done((f32[80,64]{1,0:T(8,128)S(1)}, f32[80,64]{1,0:T(8,128)}, u32[]{:S(2)}) %copy-start.4) | copy-done | bytes 20504
  5.4 0.0 copy-start.5
  5.4 0.8 %copy-done.5 = f32[64,80]{1,0:T(8,128)S(1)} copy-done((f32[64,80]{1,0:T(8,128)S(1)}, f32[64,80]{1,0:T(8,128)}, u32[]{:S(2)}) %copy-start.5) | copy-done | bytes 20504
  6.1 59.3 %shard_map.64 = f32[5,4,40,128]{3,2,1,0:T(8,128)S(1)} custom-call(f32[5,4,40,128]{3,2,1,0:T(8,128)S(1)} %copy-done.1, s32[2,4,40,128]{3,2,1,0:T(8,128)S(1)} %copy-done.2, f32[80,64]{1,0:T(8,128)S(1)} %copy-done.4, f32[64,80]{1,0:T(8,128)S(1)} %copy-done.5, f32[4,40,256]{2,1,0:T(8,128)S(1)} %copy-done.3, f32[16,4,40,256]{3,2,1,0:T(8,128)S(1)} %copy-done), custom_call_target="tpu_custom_call" | custom-call | tf_op jit(solution)/shard_map/pallas_call | solution.py:555
  65.5 0.8 %copy.8 = f32[5,4,40,128]{3,2,1,0:T(8,128)} copy(f32[5,4,40,128]{3,2,1,0:T(8,128)S(1)} %shard_map.64) | data formatting | bytes 819200
Async XLA Ops:
  0.0 1.7 %copy-start = (f32[16,4,40,256]{3,2,1,0:T(8,128)S(1)}, f32[16,4,40,256]{3,2,1,0:T(8,128)}, u32[]{:S(2)}) copy-start(f32[16,4,40,256]{3,2,1,0:T(8,128)} %constant.11.clone.band) | copy-start | bytes 7864324
  1.7 1.0 %copy-start.1 = (f32[5,4,40,128]{3,2,1,0:T(8,128)S(1)}, f32[5,4,40,128]{3,2,1,0:T(8,128)}, u32[]{:S(2)}) copy-start(f32[5,4,40,128]{3,2,1,0:T(8,128)} %state.1) | copy-start | bytes 1228804
  2.7 0.9 %copy-start.2 = (s32[2,4,40,128]{3,2,1,0:T(8,128)S(1)}, s32[2,4,40,128]{3,2,1,0:T(8,128)}, u32[]{:S(2)}) copy-start(s32[2,4,40,128]{3,2,1,0:T(8,128)} %flags.1) | copy-start | bytes 491524
  3.7 0.9 %copy-start.3 = (f32[4,40,256]{2,1,0:T(8,128)S(1)}, f32[4,40,256]{2,1,0:T(8,128)}, u32[]{:S(2)}) copy-start(f32[4,40,256]{2,1,0:T(8,128)} %constant.10.clone.twiddle) | copy-start | bytes 491524
  4.6 0.8 %copy-start.4 = (f32[80,64]{1,0:T(8,128)S(1)}, f32[80,64]{1,0:T(8,128)}, u32[]{:S(2)}) copy-start(f32[80,64]{1,0:T(8,128)} %constant.8.clone.fwd) | copy-start | bytes 61444
  5.4 0.8 %copy-start.5 = (f32[64,80]{1,0:T(8,128)S(1)}, f32[64,80]{1,0:T(8,128)}, u32[]{:S(2)}) copy-start(f32[64,80]{1,0:T(8,128)} %constant.9.clone.inv) | copy-start | bytes 61444

commit v2 on v1

--- a/solution.py
+++ b/solution.py
@@ -49,8 +49,25 @@
     return [a.astype(np.float32) for a in (fwd, inv, twiddle, band)]
 
 
-def matmul(a, b):
-    return jnp.dot(a, b, precision=lax.Precision.HIGHEST, preferred_element_type=jnp.float32)
+def split(x):
+    high = x.astype(jnp.bfloat16)
+    return high, (x - high.astype(jnp.float32)).astype(jnp.bfloat16)
+
+
+def dot(a, b):
+    return jnp.dot(a, b, preferred_element_type=jnp.float32)
+
+
+def by_left(a_high, a_low, b):
+    high, low = split(b)
+    return dot(a_high, high) + (dot(a_high, low) + dot(a_low, high))
+
+
+def by_right(a, b_high, b_low):
+    high, low = split(a)
+    rows = a.shape[0]
+    both = dot(jnp.concatenate([high, low], axis=0), b_high)
+    return both[:rows] + (both[rows:] + dot(high, b_low))
 
 
 def inverse(x):
@@ -265,9 +282,18 @@
     return [turned[48 * v : 48 * v + 48] for v in range(5)]
 
 
-def spread(send, recv, me, send_sem, recv_sem):
-    def one(i, carry):
-        to = lax.rem(me + i, 64)
+def others(me):
+    y, x, z = me // 32, lax.rem(me // 8, 4), lax.rem(me, 8)
+    ys = {d: lax.rem(y + d, 2) * 32 for d in (1, 0)}
+    xs = {d: lax.rem(x + d, 4) * 8 for d in (2, 1, 3, 0)}
+    zs = {d: lax.rem(z + d, 8) for d in (4, 3, 5, 2, 6, 1, 7, 0)}
+    steps = [(dy, dx, dz) for dz in zs for dx in xs for dy in ys]
+    steps.sort(key=lambda s: -(s[0] + min(s[1], 4 - s[1]) + min(s[2], 8 - s[2])))
+    return [ys[dy] + xs[dx] + zs[dz] for dy, dx, dz in steps[:-1]]
+
+
+def spread(send, recv, me, peers, send_sem, recv_sem):
+    for to in peers:
         pltpu.make_async_remote_copy(
             src_ref=send.at[to],
             dst_ref=recv.at[me],
@@ -276,9 +302,6 @@
             device_id={"az": to},
             device_id_type=MESH,
         ).start()
-        return carry
-
-    lax.fori_loop(1, 64, one, 0)
     recv[pl.ds(me, 1)] = send[pl.ds(me, 1)]
 
 
@@ -287,54 +310,71 @@
     pltpu.make_async_copy(rows, rows, sem).wait()
 
 
-def build_mix(mine, mix):
-    mix[...] = jnp.zeros_like(mix)
-    for part in range(2):
-        re, im = mine[2 * part], mine[2 * part + 1]
+def build_mix(mine, mix_high, mix_low):
+    mix_high[...] = jnp.zeros_like(mix_high)
+    mix_low[...] = jnp.zeros_like(mix_low)
+    for k in range(4):
+        rows = []
         for v in range(5):
-            c = pltpu.roll(re, 48 * v, 1) if v else re
-            s = pltpu.roll(im, 48 * v, 1) if v else im
-            row = 512 * part + 40 * v
-            mix[row : row + 40, :256] = c
-            mix[row : row + 40, 256:] = s
-            mix[row + 256 : row + 296, :256] = -s
-            mix[row + 256 : row + 296, 256:] = c
-
-
-def project(recv, back, me, fwd, inv, twiddle, mix):
+            rows.append(pltpu.roll(mine[k], 48 * v, 1) if v else mine[k])
+        rows.append(jnp.zeros((56, 256), jnp.float32))
+        mix_high[k], mix_low[k] = split(jnp.concatenate(rows, axis=0))
+
+
+def project(recv, back, me, fwd, inv, twiddle, mix_high, mix_low):
     x = jnp.concatenate([recv[:, 0, :], recv[:, 1, :]], axis=1)
-    a = matmul(fwd[...], x)
+    a = by_left(fwd[0], fwd[1], x)
     re, im = a[:40], a[40:]
     re, im = re * twiddle[0] - im * twiddle[1], re * twiddle[1] + im * twiddle[0]
-    special = jnp.where(lax.rem(me, 2) == 1, 0, 32)
-    own = (lax.broadcasted_iota(jnp.int32, (40, 256), 0) == special).astype(jnp.float32)
-    z = matmul(jnp.concatenate([re, im, re * own, im * own], axis=1), mix[...])
-    re, im = z[:, :256], z[:, 256:]
+    odd = lax.rem(me, 2) == 1
+    first_row = lax.broadcasted_iota(jnp.int32, (8, 256), 0) == 0
+
+    def twin_row(x):
+        return jnp.where(first_row, jnp.where(odd, x[:8], x[32:40]), 0.0)
+
+    main = jnp.concatenate([re, im], axis=0)
+    twin = jnp.concatenate([twin_row(re), twin_row(im)], axis=0)
+    c, s = by_right(main, mix_high[0], mix_low[0]), by_right(main, mix_high[1], mix_low[1])
+    tc, ts = by_right(twin, mix_high[2], mix_low[2]), by_right(twin, mix_high[3], mix_low[3])
+    re, im = c[:40] - s[40:], s[:40] + c[40:]
+    t_re, t_im = tc[:8] - ts[8:], ts[:8] + tc[8:]
+
+    def with_twin(x, t):
+        top = x[:8] + jnp.where(odd, t, 0.0)
+        return jnp.concatenate([top, x[8:32], x[32:40] + jnp.where(odd, 0.0, t)], axis=0)
+
+    re, im = with_twin(re, t_re), with_twin(im, t_im)
     re, im = re * twiddle[2] - im * twiddle[3], re * twiddle[3] + im * twiddle[2]
-    y = matmul(inv[...], jnp.concatenate([re, im], axis=0))
+    y = by_left(inv[0], inv[1], jnp.concatenate([re, im], axis=0))
     back[:, 0, :] = y[:, :128]
     back[:, 1, :] = y[:, 128:]
 
 
 def kernel(
-    state, flags, fwd, inv, twiddle, band, out,
-    mine, mix, padded, padded_flags, rate, first, second,
+    state_hbm, flags_hbm, fwd_hbm, inv_hbm, twiddle_hbm, band, out,
+    state, flags, fwd, inv, twiddle, mine, mix_high, mix_low, padded, padded_flags, rate, first, second,
     az_out, az_in, azf_out, azf_in, low, high, flow, fhigh, ghost_out, ghost_in, near_low, near_high,
     send, recv, back, ret,
     sem, az_sem, azf_sem, ax_sem, axf_sem, ghost_sem, near_sem, go_sem, come_sem,
 ):
     me, row = lax.axis_index("az"), lax.axis_index("ax")
     right, left = lax.rem(me + 1, 64), lax.rem(me + 63, 64)
-    load = pltpu.make_async_copy(band.at[lax.rem(me, 16)], mine, sem)
-    load.start()
+    pairs = [
+        (state_hbm, state),
+        (flags_hbm, flags),
+        (fwd_hbm, fwd),
+        (inv_hbm, inv),
+        (twiddle_hbm, twiddle),
+        (band.at[lax.rem(me, 16)], mine),
+    ]
+    loads = [pltpu.make_async_copy(a, b, sem.at[k]) for k, (a, b) in enumerate(pairs)]
+    for item in loads:
+        item.start()
     barrier = pltpu.get_barrier_semaphore()
 
-    def greet(i, carry):
-        peer = lax.rem(me + i, 64)
+    peers = others(me)
+    for peer in peers:
         pl.semaphore_signal(barrier, inc=1, device_id={"az": peer}, device_id_type=MESH)
-        return carry
-
-    lax.fori_loop(1, 64, greet, 0)
     for by in (1, 3):
         peer = lax.rem(row + by, 4)
         pl.semaphore_signal(barrier, inc=1, device_id={"ax": peer}, device_id_type=MESH)
@@ -384,6 +424,8 @@
         when_down(pair[0].wait_recv)
         when_up(pair[1].wait_recv)
 
+    loads[0].wait()
+    loads[1].wait()
     stage(state, az_out, 5)
     stage(flags, azf_out, 2)
     ghost_columns(state, ghost_out)
@@ -402,8 +444,9 @@
     start_ax(ax)
     start_ax(axf)
     ghost.start()
-    load.wait()
-    build_mix(mine, mix)
+    for item in loads[2:]:
+        item.wait()
+    build_mix(mine, mix_high, mix_low)
     padded[...] = jnp.zeros_like(padded)
     padded_flags[...] = jnp.zeros_like(padded_flags)
     for v in range(5):
@@ -469,7 +512,7 @@
     sent_ax(axf)
 
     to_lines(first, send.at[0])
-    spread(send.at[0], recv.at[0], me, go_sem.at[0, 0], go_sem.at[0, 1])
+    spread(send.at[0], recv.at[0], me, peers, go_sem.at[0, 0], go_sem.at[0, 1])
     stage(first, az_out, 5)
     az = az_copies(1)
     for item in az:
@@ -480,8 +523,8 @@
         for r in range(4):
             padded[v, r, 3:43] = first[v, r]
     arrived(recv.at[0], go_sem.at[0, 1])
-    project(recv.at[0], back.at[0], me, fwd, inv, twiddle, mix)
-    spread(back.at[0], ret.at[0], me, come_sem.at[0, 0], come_sem.at[0, 1])
+    project(recv.at[0], back.at[0], me, fwd, inv, twiddle, mix_high, mix_low)
+    spread(back.at[0], ret.at[0], me, peers, come_sem.at[0, 0], come_sem.at[0, 1])
     for item in az:
         item.wait_send()
         item.wait_recv()
@@ -533,33 +576,41 @@
     sent_ax(near)
 
     to_lines(second, send.at[1])
-    spread(send.at[1], recv.at[1], me, go_sem.at[1, 0], go_sem.at[1, 1])
+    spread(send.at[1], recv.at[1], me, peers, go_sem.at[1, 0], go_sem.at[1, 1])
     arrived(recv.at[1], go_sem.at[1, 1])
-    project(recv.at[1], back.at[1], me, fwd, inv, twiddle, mix)
-    spread(back.at[1], ret.at[1], me, come_sem.at[1, 0], come_sem.at[1, 1])
+    project(recv.at[1], back.at[1], me, fwd, inv, twiddle, mix_high, mix_low)
+    spread(back.at[1], ret.at[1], me, peers, come_sem.at[1, 0], come_sem.at[1, 1])
     arrived(ret.at[1], come_sem.at[1, 1])
     for r in range(4):
         blocks = from_lines(ret.at[1], 16 * r)
         for v in range(5):
-            out[v, r] = jnp.where(inner40, blocks[v][3:43], second[v, r]) - state[v, r]
+            out[v, r] = jnp.where(inner40, blocks[v][3:43], second[v, r])
     for section in range(2):
         arrived(send.at[section], go_sem.at[section, 0])
         arrived(back.at[section], come_sem.at[section, 0])
 
 
 def local(state, shock_flags):
-    tables = [jnp.asarray(t) for t in filter_tables()]
+    fwd, inv, twiddle, band = filter_tables()
+    tables = [jnp.stack(split(jnp.asarray(t))) for t in (fwd, inv)]
+    tables += [jnp.asarray(twiddle), jnp.asarray(band)]
     vmem = pl.BlockSpec(memory_space=pltpu.VMEM)
     f32, i32 = jnp.float32, jnp.int32
     dma = pltpu.SemaphoreType.DMA
-    return pl.pallas_call(
+    after = pl.pallas_call(
         kernel,
         out_shape=jax.ShapeDtypeStruct(state.shape, f32),
-        in_specs=[vmem] * 5 + [pl.BlockSpec(memory_space=pl.ANY)],
+        in_specs=[pl.BlockSpec(memory_space=pltpu.HBM)] * 6,
         out_specs=vmem,
         scratch_shapes=[
+            pltpu.VMEM((5, 4, 40, 128), f32),
+            pltpu.VMEM((2, 4, 40, 128), i32),
+            pltpu.VMEM((2, 80, 64), jnp.bfloat16),
+            pltpu.VMEM((2, 64, 80), jnp.bfloat16),
             pltpu.VMEM((4, 40, 256), f32),
-            pltpu.VMEM((1024, 512), f32),
+            pltpu.VMEM((4, 40, 256), f32),
+            pltpu.VMEM((4, 256, 256), jnp.bfloat16),
+            pltpu.VMEM((4, 256, 256), jnp.bfloat16),
             pltpu.VMEM((5, 4, 48, 128), f32),
             pltpu.VMEM((2, 4, 48, 128), f32),
             pltpu.VMEM((5, 4, 40, 128), f32),
@@ -581,7 +632,7 @@
             pltpu.VMEM((2, 64, 2, 128), f32),
             pltpu.VMEM((2, 64, 2, 128), f32),
             pltpu.VMEM((2, 64, 2, 128), f32),
-            dma,
+            dma((6,)),
             dma((2, 2, 2)),
             dma((2, 2)),
             dma((2, 2, 2)),
@@ -592,9 +643,10 @@
             dma((2, 2)),
         ],
         compiler_params=pltpu.CompilerParams(
-            collective_id=0, has_side_effects=True, vmem_limit_bytes=48 * 1024 * 1024
+            collective_id=0, has_side_effects=True, vmem_limit_bytes=63 * 1024 * 1024
         ),
     )(state, shock_flags, *tables)
+    return after - state
 
 
 def solution(mesh):

time: 66.5 us -> 56.7 us (0.85)
  local copies, waits for them, and re-layouts: 6.86 us -> 0.01 us
  Pallas kernels: 59.3 us -> 54.8 us
  other arithmetic: 0 us -> 1.8 us
    unnamed x13 -> x2, local copies, waits for them, and re-layouts: 6.86 us -> 0.01 us
    pallas_call x1, Pallas kernels: 59.3 us -> 54.8 us  [local(): pl.pallas_call(kernel, out_shape=jax.ShapeDtypeStruct(state.shape, f32),...]
    sub x0 -> x1, other arithmetic: none -> 1.8 us  [local(): return after - state]
where the time goes in v2:
time: 56.7 us; the launch traced here: 56.6 us
  Pallas kernels  54.8 us (97%)
  other arithmetic  1.8 us (3%)
    pallas_call x1, Pallas kernels, local(): pl.pallas_call(kernel, out_shape=jax.ShapeDtypeStruct(state.shape, f32),...  54.8 us
    sub x1, other arithmetic, local(): return after - state  1.8 us

profile of v2, /device:TPU:1, one launch (start us, length us, event | category | flops | bytes accessed | tf_op | source)
XLA Modules:
  0.0 56.6 jit_solution(11387933632825392165)
XLA Ops:
  0.0 0.0 copy-start
  0.0 54.8 %shard_map.64 = f32[5,4,40,128]{3,2,1,0:T(8,128)} custom-call(f32[5,4,40,128]{3,2,1,0:T(8,128)} %state_hbm.1, s32[2,4,40,128]{3,2,1,0:T(8,128)} %flags_hbm.1, bf16[2,80,64]{2,1,0:T(8,128)(2,1)} %constant.20.fwd_hbm, bf16[2,64,80]{2,1,0:T(8,128)(2,1)} %constant.27.inv_hbm, f32[4,40,256]{2,1,0:T(8,128)} %constant.10.clone.twiddle_hbm, ...), custom_call_target="tpu_custom_call" | custom-call | tf_op jit(solution)/shard_map/pallas_call | solution.py:600
  54.8 0.0 copy-done
  54.8 1.8 %sub.11 = f32[5,4,40,128]{3,2,1,0:T(8,128)} subtract(f32[5,4,40,128]{3,2,1,0:T(8,128)} %shard_map.64, f32[5,4,40,128]{3,2,1,0:T(8,128)S(1)} %copy-done) | non-fusion elementwise | flops 102400 | bytes 1228800 | tf_op jit(solution)/shard_map/sub | solution.py:649
Async XLA Ops:
  0.0 54.8 %copy-start = (f32[5,4,40,128]{3,2,1,0:T(8,128)S(1)}, f32[5,4,40,128]{3,2,1,0:T(8,128)}, u32[]{:S(2)}) copy-start(f32[5,4,40,128]{3,2,1,0:T(8,128)} %state_hbm.1) | copy-start | bytes 1228804

commit v3 on v2

--- a/solution.py
+++ b/solution.py
@@ -28,12 +28,12 @@
     scale = np.where((k1 == 0) | (k1 == 32), 1.0, 2.0)[:, None] / 2560
     for v in range(5):
         angle = 2 * np.pi * np.outer(k1, m_in) / 2560
-        twiddle[0, :33, v * 40 : v * 40 + 40] = np.cos(angle)
-        twiddle[1, :33, v * 40 : v * 40 + 40] = -np.sin(angle)
+        twiddle[0, :33, v * 48 + 3 : v * 48 + 43] = np.cos(angle)
+        twiddle[1, :33, v * 48 + 3 : v * 48 + 43] = -np.sin(angle)
         angle = 2 * np.pi * np.outer(k1, m_out) / 2560
         twiddle[2, :33, v * 48 : v * 48 + 46] = np.cos(angle) * scale
         twiddle[3, :33, v * 48 : v * 48 + 46] = np.sin(angle) * scale
-    band = np.zeros((16, 4, 40, 256))
+    band = np.zeros((16, 4, 48, 256))
     delta = m_out[None, :] - m_in[:, None]
     for j in range(16):
         if j % 2:
@@ -44,8 +44,8 @@
             modes, extra = np.arange(-q, q + 1), q
         kept = sum(np.exp(2j * np.pi * k * delta / 40) for k in modes)
         twin = np.exp(2j * np.pi * extra * delta / 40)
-        band[j, 0, :, :46], band[j, 1, :, :46] = kept.real, kept.imag
-        band[j, 2, :, :46], band[j, 3, :, :46] = twin.real, twin.imag
+        for k, part in enumerate((kept.real, kept.imag, twin.real, twin.imag)):
+            band[j, k, 3:43, :46] = part
     return [a.astype(np.float32) for a in (fwd, inv, twiddle, band)]
 
 
@@ -104,8 +104,9 @@
 def at(x, by):
     if isinstance(x, Rows):
         return x.shifted(by)
-    n = x.shape[0]
-    return pltpu.roll(x, (n - by) % n, 0)
+    axis = 1 if x.shape[1] == 256 else 0
+    n = x.shape[axis]
+    return pltpu.roll(x, (n - by) % n, axis)
 
 
 def inverse_of(x):
@@ -203,10 +204,9 @@
     lax.fori_loop(0, 4, row, 0)
 
 
-def finish(own, low, high, flags, flags_low, flags_high, section, ghost, rate, combine):
+def finish(own, low, high, flags, flags_low, flags_high, section, rate, combine):
     inv_r = 1.0 / radius(8)
     lane = lanes((8, 128))
-    signs = [1.0, 1.0, -1.0, -1.0, 1.0]
 
     def chunk(c, carry):
         at8 = pl.ds(pl.multiple_of(c * 8, 8), 8)
@@ -227,21 +227,16 @@
         inv_rho = u[0].map(inverse)
         p = pressure(u, inv_rho)
         f = fluxes(u, u[1] * inv_rho, p, 0)
-        columns = ghost[at8, :]
         radial, source = [], []
         for r in range(4):
             here = [u[v].cells[3 + r] for v in range(5)]
-            there = [pltpu.roll(columns, (128 - (v * 4 + r)) % 128, 1) * signs[v] for v in range(5)]
-            there[0] = jnp.where(lane == 0, there[0], 1.0)
-            there_inv = inverse(there[0])
-            g_ghost = fluxes(there, there[2] * there_inv, pressure(there, there_inv), 1)
             inv_here, p_here = inv_rho.cells[3 + r], p.cells[3 + r]
             g = fluxes(here, here[2] * inv_here, p_here, 1)
             swirl = here[3] * inv_here
             extra = [None, None, here[3] * swirl + p_here, -here[2] * swirl, None]
             terms = []
             for v in range(5):
-                before = jnp.where(lane == 0, g_ghost[v], pltpu.roll(g[v], 1, 1))
+                before = pltpu.roll(g[v], 1, 1)
                 after = jnp.where(lane == 127, g[v], pltpu.roll(g[v], 127, 1))
                 away = g[v] if extra[v] is None else g[v] - extra[v]
                 terms.append((after - before) * 0.5 + away * inv_r)
@@ -256,30 +251,155 @@
     lax.fori_loop(0, 5, chunk, 0)
 
 
-def ghost_columns(field, staging):
-    lane = lanes((40, 128))
-    packed = jnp.zeros((40, 128), jnp.float32)
-    for v in range(5):
-        for r in range(4):
-            k = v * 4 + r
-            value = field[v, r]
-            packed = jnp.where(lane == k, pltpu.roll(value, k, 1) if k else value, packed)
-    staging[...] = packed
-
-
-def to_lines(field, send):
-    for r in range(4):
-        stack = [field[v, r] for v in range(5)] + [jnp.zeros((56, 128), jnp.float32)]
-        turned = jnp.transpose(jnp.concatenate(stack, axis=0))[:16]
-        send[16 * r : 16 * r + 16, 0, :] = turned[:, :128]
-        send[16 * r : 16 * r + 16, 1, :] = turned[:, 128:]
-
-
-def from_lines(ret, first):
-    lines = jnp.concatenate([ret[first : first + 16, 0, :], ret[first : first + 16, 1, :]], axis=1)
-    lines = jnp.concatenate([lines, jnp.zeros((112, 256), jnp.float32)], axis=0)
+def cell_of(width):
+    return lax.rem(lanes((16, width)), 48)
+
+
+def side_by_side(blocks):
+    lane = lanes(blocks[0].shape)
+    packed = blocks[0]
+    for r in range(1, 4):
+        packed = jnp.where(lane >= 32 * r, pltpu.roll(blocks[r], 32 * r, 1), packed)
+    return packed
+
+
+def pack_state(padded):
+    stacks = []
+    for r in range(4):
+        rest = jnp.zeros((16, 128), jnp.float32)
+        stacks.append(jnp.concatenate([padded[v, r] for v in range(5)] + [rest], axis=0))
+    return jnp.transpose(side_by_side(stacks))
+
+
+def pack_flags(padded_flags):
+    stacks = []
+    for r in range(4):
+        rest = jnp.zeros((32, 128), jnp.float32)
+        stacks.append(jnp.concatenate([padded_flags[0, r], padded_flags[1, r], rest], axis=0))
+    return jnp.transpose(side_by_side(stacks))
+
+
+def fold_ends(blocks, width):
+    cell = cell_of(width)
+    to_right = jnp.zeros((16, width), jnp.float32)
+    to_left = to_right
+    for r in range(4):
+        moved = pltpu.roll(blocks[r], (width - 40 + 3 * r) % width, 1)
+        to_right = jnp.where((cell >= 3 * r) & (cell < 3 * r + 3), moved, to_right)
+        moved = pltpu.roll(blocks[r], 31 + 3 * r, 1)
+        to_left = jnp.where((cell >= 34 + 3 * r) & (cell < 37 + 3 * r), moved, to_left)
+    return to_right, to_left
+
+
+def with_ends(block, from_left, from_right, r):
+    width = block.shape[1]
+    cell = cell_of(width)
+    before = pltpu.roll(from_left, width - 3 * r, 1) if r else from_left
+    after = pltpu.roll(from_right, 9 - 3 * r, 1) if r < 3 else from_right
+    return jnp.where(cell < 3, before, jnp.where(cell < 43, block, jnp.where(cell < 46, after, 0.0)))
+
+
+def replicate(x):
+    x = jnp.where(lanes(x.shape) < 48, x, 0.0)
+    one = jnp.concatenate([x, jnp.zeros_like(x)], axis=1)
+    two = one + pltpu.roll(one, 48, 1)
+    four = two + pltpu.roll(two, 96, 1)
+    return four + pltpu.roll(one, 192, 1)
+
+
+def primitives(u):
+    parts = [u[:, :128]] + [pltpu.roll(u, 256 - 48 * k, 1)[:, :128] for k in range(1, 5)]
+    inv_rho = inverse(parts[0])
+    return parts, inv_rho, pressure(parts, inv_rho)
+
+
+def slot(shape, k):
+    lane = lanes(shape)
+    return (lane >= 48 * k) & (lane < 48 * k + 48)
+
+
+def packed_flux(u, q, p, component):
+    own, energy = slot(u.shape, 1 + component), slot(u.shape, 4)
+    return u * q + jnp.where(own, p, jnp.where(energy, p * q, 0.0))
+
+
+def near_azimuthal(own, marks, section, rate):
+    for r in range(4):
+        u = own(r)
+        parts, inv_rho, p = primitives(u)
+        q = replicate(parts[3] * inv_rho)
+        f = packed_flux(u, q, replicate(p), 2)
+        mark = marks(r)
+        switch = window(replicate(pltpu.roll(mark, 80, 1) if section else mark))
+        face = faces(f, u, switch, pick)
+        cycle = lax.broadcasted_iota(jnp.int32, (16, 256), 0).astype(jnp.float32) + 0.5
+        rate[16 * r : 16 * r + 16, :] = (at(face, -1) - face) * (1.0 / (cycle * (2.0 * math.pi / 2560)))
+
+
+def near_finish(low, own, high, outer, ghost, marks, section, rate, combine):
+    blocks = [low(k) for k in range(3)] + [own(r) for r in range(4)] + [high(k) for k in range(3)]
+    f, switches, radial = [], [], []
+    for k, u in enumerate(blocks):
+        parts, inv_rho, p = primitives(u)
+        wide_p = replicate(p)
+        f.append(packed_flux(u, replicate(parts[1] * inv_rho), wide_p, 0))
+        mark = marks[k]
+        switches.append(replicate(pltpu.roll(mark, 80, 1) if section else mark))
+        if 3 <= k < 7:
+            r = k - 3
+            beyond = outer(r)
+            row = lax.broadcasted_iota(jnp.int32, (8, 256), 0)
+            negated = slot((8, 256), 2) | slot((8, 256), 3)
+            mirror = jnp.broadcast_to(ghost(r), (8, 256))
+            mirror = jnp.where(negated, -mirror, mirror)
+            beyond = jnp.where(row == 7, mirror, beyond)
+            b_parts, b_inv, b_p = primitives(beyond)
+            g_beyond = packed_flux(beyond, replicate(b_parts[2] * b_inv), replicate(b_p), 1)
+            g = packed_flux(u, replicate(parts[2] * inv_rho), wide_p, 1)
+            q_t = replicate(parts[3] * inv_rho)
+            extra = jnp.where(
+                slot((16, 256), 2),
+                pltpu.roll(u, 256 - 48, 1) * q_t + wide_p,
+                jnp.where(slot((16, 256), 3), -pltpu.roll(u, 48, 1) * q_t, 0.0),
+            )
+            ring = jnp.concatenate([g, g_beyond], axis=0)
+            after, before = pltpu.roll(ring, 23, 0)[:16], pltpu.roll(ring, 1, 0)[:16]
+            cycle = lax.broadcasted_iota(jnp.int32, (16, 256), 0).astype(jnp.float32) + 0.5
+            radial.append((after - before) * 0.5 + (g - extra) * (1.0 / cycle))
+    slopes = [[[None, None], [None, None]] for _ in range(4)]
+    for h in range(2):
+        for w in range(2):
+            part = (slice(8 * h, 8 * h + 8), slice(128 * w, 128 * w + 128))
+            face = faces(
+                Rows([x[part] for x in f]),
+                Rows([x[part] for x in blocks]),
+                window(Rows([x[part] for x in switches])),
+                pick,
+            ).cells
+            for r in range(4):
+                slopes[r][h][w] = face[2 + r] - face[3 + r]
+    lane = lanes((16, 256))
+    cell = lax.rem(lane, 48)
+    valid = (cell >= 3) & (cell < 43) & (lane < 240)
+    for r in range(4):
+        rows = [jnp.concatenate(pair, axis=1) for pair in slopes[r]]
+        slope = jnp.concatenate(rows, axis=0) - radial[r] + rate[16 * r : 16 * r + 16, :]
+        combine(r, jnp.where(valid, slope, 0.0), valid)
+
+
+def packed_rows(ref, first, count):
+    return jnp.concatenate([ref[first : first + count, 0, :], ref[first : first + count, 1, :]], axis=1)
+
+
+def unpack(ret):
+    lines = jnp.concatenate([packed_rows(ret, 0, 64), jnp.zeros((64, 256), jnp.float32)], axis=0)
     turned = jnp.transpose(lines)
-    return [turned[48 * v : 48 * v + 48] for v in range(5)]
+
+    def block(v, r):
+        rows = turned[48 * v : 48 * v + 48]
+        return pltpu.roll(rows, 128 - 16 * r, 1) if r else rows
+
+    return block
 
 
 def others(me):
@@ -317,7 +437,7 @@
         rows = []
         for v in range(5):
             rows.append(pltpu.roll(mine[k], 48 * v, 1) if v else mine[k])
-        rows.append(jnp.zeros((56, 256), jnp.float32))
+        rows.append(jnp.zeros((16, 256), jnp.float32))
         mix_high[k], mix_low[k] = split(jnp.concatenate(rows, axis=0))
 
 
@@ -353,12 +473,17 @@
 def kernel(
     state_hbm, flags_hbm, fwd_hbm, inv_hbm, twiddle_hbm, band, out,
     state, flags, fwd, inv, twiddle, mine, mix_high, mix_low, padded, padded_flags, rate, first, second,
-    az_out, az_in, azf_out, azf_in, low, high, flow, fhigh, ghost_out, ghost_in, near_low, near_high,
+    az_out, az_in, azf_out, azf_in, low, high, flow, fhigh,
+    near, near_rate, near_low, near_high, near_outer, ends_out, ends_in, marks, marks_low, marks_high,
+    mark_ends_out, mark_ends_in, ghost_out, ghost_in, near2_low, near2_high,
     send, recv, back, ret,
-    sem, az_sem, azf_sem, ax_sem, axf_sem, ghost_sem, near_sem, go_sem, come_sem,
+    sem, az_sem, azf_sem, ax_sem, axf_sem, end_sem, mark_end_sem, row_sem, mark_row_sem, ghost_sem, near_sem,
+    go_sem, come_sem,
 ):
     me, row = lax.axis_index("az"), lax.axis_index("ax")
     right, left = lax.rem(me + 1, 64), lax.rem(me + 63, 64)
+    upper, lower = lax.rem(row + 1, 4), lax.rem(row + 3, 4)
+    opposite = lax.rem(me + 32, 64)
     pairs = [
         (state_hbm, state),
         (flags_hbm, flags),
@@ -371,12 +496,10 @@
     for item in loads:
         item.start()
     barrier = pltpu.get_barrier_semaphore()
-
     peers = others(me)
     for peer in peers:
         pl.semaphore_signal(barrier, inc=1, device_id={"az": peer}, device_id_type=MESH)
-    for by in (1, 3):
-        peer = lax.rem(row + by, 4)
+    for peer in (upper, lower):
         pl.semaphore_signal(barrier, inc=1, device_id={"ax": peer}, device_id_type=MESH)
 
     def copy(src, dst, sems, k, **place):
@@ -389,16 +512,17 @@
             device_id_type=MESH,
         )
 
-    def az_copies(section):
+    def along_az(source, target, sems):
         return [
-            copy(az_out.at[0], az_in.at[section, 0], az_sem.at[section], 0, az=right),
-            copy(az_out.at[1], az_in.at[section, 1], az_sem.at[section], 1, az=left),
+            copy(source.at[0], target.at[0], sems, 0, az=right),
+            copy(source.at[1], target.at[1], sems, 1, az=left),
         ]
 
-    def ax_copies(field, to_low, to_high, sems):
-        up = copy(field.at[:, pl.ds(1, 3)], to_low, sems, 0, ax=lax.rem(row + 1, 4))
-        down = copy(field.at[:, pl.ds(0, 3)], to_high, sems, 1, ax=lax.rem(row + 3, 4))
-        return up, down
+    def along_ax(up_from, to_low, down_from, to_high, sems):
+        return copy(up_from, to_low, sems, 0, ax=upper), copy(down_from, to_high, sems, 1, ax=lower)
+
+    def wide_ax(field, to_low, to_high, sems):
+        return along_ax(field.at[:, pl.ds(1, 3)], to_low, field.at[:, pl.ds(0, 3)], to_high, sems)
 
     def stage(field, staging, fields):
         for f in range(fields):
@@ -424,37 +548,129 @@
         when_down(pair[0].wait_recv)
         when_up(pair[1].wait_recv)
 
+    def start_all(items):
+        for item in items:
+            item.start()
+
+    def came_all(items):
+        for item in items:
+            item.wait_recv()
+
+    def sent_all(items):
+        for item in items:
+            item.wait_send()
+
+    padded[...] = jnp.zeros_like(padded)
+    padded_flags[...] = jnp.zeros_like(padded_flags)
     loads[0].wait()
     loads[1].wait()
-    stage(state, az_out, 5)
-    stage(flags, azf_out, 2)
-    ghost_columns(state, ghost_out)
-    az = az_copies(0)
-    azf = [
-        copy(azf_out.at[0], azf_in.at[0], azf_sem, 0, az=right),
-        copy(azf_out.at[1], azf_in.at[1], azf_sem, 1, az=left),
-    ]
-    opposite = lax.rem(me + 32, 64)
-    ghost = copy(ghost_out, ghost_in.at[0], ghost_sem.at[0], 0, az=opposite)
-    ax = ax_copies(state, low.at[0], high.at[0], ax_sem.at[0])
-    axf = ax_copies(flags, flow, fhigh, axf_sem)
-    pl.semaphore_wait(barrier, 65)
-    for item in az + azf:
-        item.start()
-    start_ax(ax)
-    start_ax(axf)
-    ghost.start()
-    for item in loads[2:]:
-        item.wait()
-    build_mix(mine, mix_high, mix_low)
-    padded[...] = jnp.zeros_like(padded)
-    padded_flags[...] = jnp.zeros_like(padded_flags)
     for v in range(5):
         for r in range(4):
             padded[v, r, 3:43] = state[v, r]
     for s in range(2):
         for r in range(4):
             padded_flags[s, r, 3:43] = flags[s, r].astype(jnp.float32)
+    packed = pack_state(padded)
+    for r in range(4):
+        near[0, 16 * r : 16 * r + 16, :] = packed[32 * r : 32 * r + 16]
+        near_outer[0, 8 * r : 8 * r + 8, :] = packed[32 * r + 16 : 32 * r + 24]
+        ghost_out[0, r, 0:1, :] = packed[32 * r : 32 * r + 1, :128]
+        ghost_out[0, r, 1:2, :] = packed[32 * r : 32 * r + 1, 128:]
+    ends_out[0], ends_out[1] = fold_ends([packed[32 * r : 32 * r + 16] for r in range(4)], 256)
+    packed = pack_flags(padded_flags)
+    for r in range(4):
+        marks[0, 16 * r : 16 * r + 16, :] = packed[32 * r : 32 * r + 16]
+    mark_ends_out[0], mark_ends_out[1] = fold_ends([packed[32 * r : 32 * r + 16] for r in range(4)], 128)
+    ends = along_az(ends_out, ends_in, end_sem)
+    mark_ends = along_az(mark_ends_out, mark_ends_in, mark_end_sem)
+    rows = along_ax(near.at[0, pl.ds(16, 48)], near_low, near.at[0, pl.ds(0, 48)], near_high, row_sem)
+    mark_rows = along_ax(marks.at[0, pl.ds(16, 48)], marks_low, marks.at[0, pl.ds(0, 48)], marks_high, mark_row_sem)
+    ghost = copy(ghost_out.at[0], ghost_in.at[0], ghost_sem.at[0], 0, az=opposite)
+    stage(state, az_out, 5)
+    stage(flags, azf_out, 2)
+    az = along_az(az_out, az_in.at[0], az_sem.at[0])
+    azf = along_az(azf_out, azf_in, azf_sem)
+    ax = wide_ax(state, low.at[0], high.at[0], ax_sem.at[0])
+    axf = wide_ax(flags, flow, fhigh, axf_sem)
+    pl.semaphore_wait(barrier, 65)
+    start_ax(rows)
+    start_all(ends)
+    ghost.start()
+    start_all(mark_ends)
+    start_ax(mark_rows)
+    start_all(az)
+    start_all(azf)
+    start_ax(ax)
+    start_ax(axf)
+    for item in loads[2:]:
+        item.wait()
+    build_mix(mine, mix_high, mix_low)
+
+    came_all(ends)
+    came_all(mark_ends)
+    for r in range(4):
+        at_row = slice(16 * r, 16 * r + 16)
+        near[1, at_row, :] = with_ends(near[0, at_row, :], ends_in[0], ends_in[1], r)
+        marks[1, at_row, :] = with_ends(marks[0, at_row, :], mark_ends_in[0], mark_ends_in[1], r)
+
+    def own_state(r):
+        return near[1, 16 * r : 16 * r + 16, :]
+
+    def own_marks(r):
+        return marks[1, 16 * r : 16 * r + 16, :]
+
+    near_azimuthal(own_state, own_marks, 0, near_rate)
+    came_ax(rows)
+    came_ax(mark_rows)
+
+    def low_rim():
+        for k in range(3):
+            near_low[16 * k : 16 * k + 16, :] = near[1, 0:16, :]
+            marks_low[16 * k : 16 * k + 16, :] = marks[1, 0:16, :]
+
+    def high_rim():
+        for k in range(3):
+            near_high[16 * k : 16 * k + 16, :] = near[1, 48:64, :]
+            marks_high[16 * k : 16 * k + 16, :] = marks[1, 48:64, :]
+
+    pl.when(row == 0)(low_rim)
+    pl.when(row == 3)(high_rim)
+    ghost.wait_recv()
+
+    def mark_list():
+        below = [marks_low[16 * k : 16 * k + 16, :] for k in range(3)]
+        above = [marks_high[16 * k : 16 * k + 16, :] for k in range(3)]
+        return below + [own_marks(r) for r in range(4)] + above
+
+    def ghost_row(section):
+        return lambda r: jnp.concatenate([ghost_in[section, r, 0:1, :], ghost_in[section, r, 1:2, :]], axis=1)
+
+    def outer_rows(section):
+        return lambda r: near_outer[section, 8 * r : 8 * r + 8, :]
+
+    def hand_in(section, r, value):
+        send[section, 16 * r : 16 * r + 16, 0, :] = value[:, :128]
+        send[section, 16 * r : 16 * r + 16, 1, :] = value[:, 128:]
+
+    def near_first(r, slope, valid):
+        hand_in(0, r, jnp.where(valid, own_state(r) + slope * time_step, 0.0))
+
+    near_finish(
+        lambda k: near_low[16 * k : 16 * k + 16, :],
+        own_state,
+        lambda k: near_high[16 * k : 16 * k + 16, :],
+        outer_rows(0),
+        ghost_row(0),
+        mark_list(),
+        0,
+        near_rate,
+        near_first,
+    )
+    spread(send.at[0], recv.at[0], me, peers, go_sem.at[0, 0], go_sem.at[0, 1])
+
+    sent_ax(rows)
+    sent_ax(mark_rows)
+    sent_all(ends + mark_ends + [ghost])
 
     def fill_az(section):
         for v in range(5):
@@ -462,9 +678,8 @@
                 padded[v, r, 0:3] = az_in[section, 0, v * 4 + r, 0:3]
                 padded[v, r, 43:46] = az_in[section, 1, v * 4 + r, 0:3]
 
-    for item in az + azf:
-        item.wait_send()
-        item.wait_recv()
+    came_all(az)
+    came_all(azf)
     fill_az(0)
     for s in range(2):
         for r in range(4):
@@ -501,93 +716,102 @@
     rims(state, 0)
     pl.when(row == 0)(flag_low_rim)
     pl.when(row == 3)(flag_high_rim)
-    ghost.wait_send()
-    ghost.wait_recv()
 
     def combine_first(v, r, rows, here, slope):
         first[v, r, rows, :] = here + slope * time_step
 
-    finish(state, low.at[0], high.at[0], flags, flow, fhigh, 0, ghost_in.at[0], rate, combine_first)
-    sent_ax(ax)
-    sent_ax(axf)
-
-    to_lines(first, send.at[0])
-    spread(send.at[0], recv.at[0], me, peers, go_sem.at[0, 0], go_sem.at[0, 1])
+    finish(state, low.at[0], high.at[0], flags, flow, fhigh, 0, rate, combine_first)
+    sent_all(az + azf)
+    arrived(recv.at[0], go_sem.at[0, 1])
+    project(recv.at[0], back.at[0], me, fwd, inv, twiddle, mix_high, mix_low)
+    spread(back.at[0], ret.at[0], me, peers, come_sem.at[0, 0], come_sem.at[0, 1])
     stage(first, az_out, 5)
-    az = az_copies(1)
-    for item in az:
-        item.start()
-    ax = ax_copies(first, low.at[1], high.at[1], ax_sem.at[1])
-    start_ax(ax)
+    az = along_az(az_out, az_in.at[1], az_sem.at[1])
+    start_all(az)
+    ax2 = wide_ax(first, low.at[1], high.at[1], ax_sem.at[1])
+    start_ax(ax2)
     for v in range(5):
         for r in range(4):
             padded[v, r, 3:43] = first[v, r]
-    arrived(recv.at[0], go_sem.at[0, 1])
-    project(recv.at[0], back.at[0], me, fwd, inv, twiddle, mix_high, mix_low)
-    spread(back.at[0], ret.at[0], me, peers, come_sem.at[0, 0], come_sem.at[0, 1])
-    for item in az:
-        item.wait_send()
-        item.wait_recv()
+    packed = pack_state(padded)
+    for r in range(4):
+        near_outer[1, 8 * r : 8 * r + 8, :] = packed[32 * r + 16 : 32 * r + 24]
+    arrived(ret.at[0], come_sem.at[0, 1])
+
+    rows = along_ax(ret.at[0, pl.ds(16, 48)], near2_low, ret.at[0, pl.ds(0, 48)], near2_high, near_sem)
+    start_ax(rows)
+    for r in range(4):
+        ghost_out[1, r] = ret[0, 16 * r]
+    ghost = copy(ghost_out.at[1], ghost_in.at[1], ghost_sem.at[1], 0, az=opposite)
+    ghost.start()
+
+    def own_first(r):
+        return packed_rows(ret.at[0], 16 * r, 16)
+
+    near_azimuthal(own_first, own_marks, 1, near_rate)
+    came_ax(rows)
+
+    def low_rim_two():
+        for k in range(3):
+            near2_low[16 * k : 16 * k + 16] = ret[0, 0:16]
+
+    def high_rim_two():
+        for k in range(3):
+            near2_high[16 * k : 16 * k + 16] = ret[0, 48:64]
+
+    pl.when(row == 0)(low_rim_two)
+    pl.when(row == 3)(high_rim_two)
+    ghost.wait_recv()
+
+    def near_second(r, slope, valid):
+        value = own_state(r) * 0.75 + (own_first(r) + slope * time_step) * 0.25
+        hand_in(1, r, jnp.where(valid, value, 0.0))
+
+    near_finish(
+        lambda k: packed_rows(near2_low, 16 * k, 16),
+        own_first,
+        lambda k: packed_rows(near2_high, 16 * k, 16),
+        outer_rows(1),
+        ghost_row(1),
+        mark_list(),
+        1,
+        near_rate,
+        near_second,
+    )
+    spread(send.at[1], recv.at[1], me, peers, go_sem.at[1, 0], go_sem.at[1, 1])
+
+    inner40 = lanes((40, 128)) < NRING
+    sent_ax(ax)
+    sent_ax(axf)
+    sent_ax(ax2)
+    block = unpack(ret.at[0])
+    for r in range(4):
+        for v in range(5):
+            first[v, r] = jnp.where(inner40, block(v, r)[3:43], first[v, r])
+    came_all(az)
+    sent_all(az + [ghost])
     fill_az(1)
-    sent_ax(ax)
-    came_ax(ax)
-    arrived(ret.at[0], come_sem.at[0, 1])
-
-    near = (
-        copy(ret.at[0, pl.ds(16, 48)], near_low, near_sem, 0, ax=lax.rem(row + 1, 4)),
-        copy(ret.at[0, pl.ds(0, 48)], near_high, near_sem, 1, ax=lax.rem(row + 3, 4)),
-    )
-    start_ax(near)
-    inner48, inner40 = lanes((48, 128)) < NRING, lanes((40, 128)) < NRING
-    for r in range(4):
-        blocks = from_lines(ret.at[0], 16 * r)
-        for v in range(5):
-            merged = jnp.where(inner48, blocks[v], padded[v, r])
-            padded[v, r] = merged
-            first[v, r] = merged[3:43]
-    ghost_columns(first, ghost_out)
-    ghost = copy(ghost_out, ghost_in.at[1], ghost_sem.at[1], 0, az=opposite)
-    ghost.start()
     azimuthal(padded, padded_flags, 1, rate)
-    came_ax(near)
-
-    def merge_low():
-        for k in range(3):
-            blocks = from_lines(near_low, 16 * k)
-            for v in range(5):
-                low[1, v, k] = jnp.where(inner40, blocks[v][3:43], low[1, v, k])
-
-    def merge_high():
-        for k in range(3):
-            blocks = from_lines(near_high, 16 * k)
-            for v in range(5):
-                high[1, v, k] = jnp.where(inner40, blocks[v][3:43], high[1, v, k])
-
-    when_down(merge_low)
-    when_up(merge_high)
-    rims(first, 1)
-    ghost.wait_send()
-    ghost.wait_recv()
-
-    def combine_second(v, r, rows, here, slope):
-        second[v, r, rows, :] = state[v, r, rows, :] * 0.75 + (here + slope * time_step) * 0.25
-
-    finish(first, low.at[1], high.at[1], flags, flow, fhigh, 1, ghost_in.at[1], rate, combine_second)
-    sent_ax(near)
-
-    to_lines(second, send.at[1])
-    spread(send.at[1], recv.at[1], me, peers, go_sem.at[1, 0], go_sem.at[1, 1])
     arrived(recv.at[1], go_sem.at[1, 1])
     project(recv.at[1], back.at[1], me, fwd, inv, twiddle, mix_high, mix_low)
     spread(back.at[1], ret.at[1], me, peers, come_sem.at[1, 0], come_sem.at[1, 1])
-    arrived(ret.at[1], come_sem.at[1, 1])
-    for r in range(4):
-        blocks = from_lines(ret.at[1], 16 * r)
-        for v in range(5):
-            out[v, r] = jnp.where(inner40, blocks[v][3:43], second[v, r])
+    came_ax(ax2)
+    rims(first, 1)
+
+    def combine_second(v, r, rows, here, slope):
+        second[v, r, rows, :] = state[v, r, rows, :] * 0.75 + (here + slope * time_step) * 0.25
+
+    finish(first, low.at[1], high.at[1], flags, flow, fhigh, 1, rate, combine_second)
+    sent_ax(rows)
     for section in range(2):
         arrived(send.at[section], go_sem.at[section, 0])
-        arrived(back.at[section], come_sem.at[section, 0])
+    arrived(back.at[0], come_sem.at[0, 0])
+    arrived(ret.at[1], come_sem.at[1, 1])
+    block = unpack(ret.at[1])
+    for r in range(4):
+        for v in range(5):
+            out[v, r] = jnp.where(inner40, block(v, r)[3:43], second[v, r])
+    arrived(back.at[1], come_sem.at[1, 0])
 
 
 def local(state, shock_flags):
@@ -597,6 +821,7 @@
     vmem = pl.BlockSpec(memory_space=pltpu.VMEM)
     f32, i32 = jnp.float32, jnp.int32
     dma = pltpu.SemaphoreType.DMA
+    in_hbm = [pltpu.with_memory_space_constraint(x, pltpu.HBM) for x in (state, shock_flags, *tables)]
     after = pl.pallas_call(
         kernel,
         out_shape=jax.ShapeDtypeStruct(state.shape, f32),
@@ -608,7 +833,7 @@
             pltpu.VMEM((2, 80, 64), jnp.bfloat16),
             pltpu.VMEM((2, 64, 80), jnp.bfloat16),
             pltpu.VMEM((4, 40, 256), f32),
-            pltpu.VMEM((4, 40, 256), f32),
+            pltpu.VMEM((4, 48, 256), f32),
             pltpu.VMEM((4, 256, 256), jnp.bfloat16),
             pltpu.VMEM((4, 256, 256), jnp.bfloat16),
             pltpu.VMEM((5, 4, 48, 128), f32),
@@ -624,8 +849,20 @@
             pltpu.VMEM((2, 5, 3, 40, 128), f32),
             pltpu.VMEM((2, 3, 40, 128), i32),
             pltpu.VMEM((2, 3, 40, 128), i32),
-            pltpu.VMEM((40, 128), f32),
-            pltpu.VMEM((2, 40, 128), f32),
+            pltpu.VMEM((2, 64, 256), f32),
+            pltpu.VMEM((64, 256), f32),
+            pltpu.VMEM((48, 256), f32),
+            pltpu.VMEM((48, 256), f32),
+            pltpu.VMEM((2, 32, 256), f32),
+            pltpu.VMEM((2, 16, 256), f32),
+            pltpu.VMEM((2, 16, 256), f32),
+            pltpu.VMEM((2, 64, 128), f32),
+            pltpu.VMEM((48, 128), f32),
+            pltpu.VMEM((48, 128), f32),
+            pltpu.VMEM((2, 16, 128), f32),
+            pltpu.VMEM((2, 16, 128), f32),
+            pltpu.VMEM((2, 4, 2, 128), f32),
+            pltpu.VMEM((2, 4, 2, 128), f32),
             pltpu.VMEM((48, 2, 128), f32),
             pltpu.VMEM((48, 2, 128), f32),
             pltpu.VMEM((2, 64, 2, 128), f32),
@@ -637,15 +874,19 @@
             dma((2, 2)),
             dma((2, 2, 2)),
             dma((2, 2)),
+            dma((2, 2)),
+            dma((2, 2)),
+            dma((2, 2)),
+            dma((2, 2)),
             dma((2, 2, 1)),
             dma((2, 2)),
             dma((2, 2)),
             dma((2, 2)),
         ],
         compiler_params=pltpu.CompilerParams(
-            collective_id=0, has_side_effects=True, vmem_limit_bytes=63 * 1024 * 1024
+            collective_id=0, has_side_effects=True, vmem_limit_bytes=40 * 1024 * 1024
         ),
-    )(state, shock_flags, *tables)
+    )(*in_hbm)
     return after - state
 
 

time: 56.7 us -> 49.1 us (0.87)
  Pallas kernels: 54.8 us -> 48.2 us
  other arithmetic: 1.8 us -> 0.8 us
    pallas_call x1, Pallas kernels: 54.8 us -> 48.2 us  [local(): pl.pallas_call(kernel, out_shape=jax.ShapeDtypeStruct(state.shape, f32),...]
    sub x1, other arithmetic: 1.8 us -> 0.8 us  [local(): return after - state]
where the time goes in v3:
time: 49.1 us; the launch traced here: 49 us
  Pallas kernels  48.2 us (98%)
  other arithmetic  0.8 us (2%)
    pallas_call x1, Pallas kernels, local(): pl.pallas_call(kernel, out_shape=jax.ShapeDtypeStruct(state.shape, f32),...  48.2 us

profile of v3, /device:TPU:1, one launch (start us, length us, event | category | flops | bytes accessed | tf_op | source)
XLA Modules:
  0.0 49.0 jit_solution(12080826303940228985)
XLA Ops:
  0.0 0.0 copy-start
  0.0 48.2 %shard_map.64 = f32[5,4,40,128]{3,2,1,0:T(8,128)S(1)} custom-call(f32[5,4,40,128]{3,2,1,0:T(8,128)} %state_hbm.1, s32[2,4,40,128]{3,2,1,0:T(8,128)} %flags_hbm.1, bf16[2,80,64]{2,1,0:T(8,128)(2,1)} %constant.20.fwd_hbm, bf16[2,64,80]{2,1,0:T(8,128)(2,1)} %constant.27.inv_hbm, f32[4,40,256]{2,1,0:T(8,128)} %constant.10.clone.twiddle_hbm, ...), custom_call_target="tpu_custom_call" | custom-call | tf_op jit(solution)/shard_map/pallas_call | solution.py:825
  48.2 0.0 copy-done
  48.2 0.8 %sub.11 = f32[5,4,40,128]{3,2,1,0:T(8,128)} subtract(f32[5,4,40,128]{3,2,1,0:T(8,128)S(1)} %shard_map.64, f32[5,4,40,128]{3,2,1,0:T(8,128)S(1)} %copy-done) | non-fusion elementwise | flops 102400 | bytes 1228800 | tf_op jit(solution)/shard_map/sub | solution.py:890
Async XLA Ops:
  0.0 48.2 %copy-start = (f32[5,4,40,128]{3,2,1,0:T(8,128)S(1)}, f32[5,4,40,128]{3,2,1,0:T(8,128)}, u32[]{:S(2)}) copy-start(f32[5,4,40,128]{3,2,1,0:T(8,128)} %state_hbm.1) | copy-start | bytes 1228804

commit v4 on v3

--- a/solution.py
+++ b/solution.py
@@ -724,7 +724,36 @@
     sent_all(az + azf)
     arrived(recv.at[0], go_sem.at[0, 1])
     project(recv.at[0], back.at[0], me, fwd, inv, twiddle, mix_high, mix_low)
-    spread(back.at[0], ret.at[0], me, peers, come_sem.at[0, 0], come_sem.at[0, 1])
+    places = peers + [me]
+    owner_row = me // 16
+    leads_up, leads_down = (row < 3) & (owner_row > 0), (row > 0) & (owner_row < 3)
+    leads_ghost = lax.rem(me, 16) == 0
+
+    def hand_out(places):
+        for to in places:
+            copy(back.at[0, to], ret.at[0, me], come_sem, 0, az=to).start()
+
+    def hand_up(places):
+        for to in places:
+            copy(back.at[0, to], near2_low.at[me - 16], near_sem, 0, ax=upper, az=to).start()
+
+    def hand_down(places):
+        for to in places:
+            copy(back.at[0, to], near2_high.at[me], near_sem, 1, ax=lower, az=to).start()
+
+    def hand_ghost():
+        for to in peers:
+            copy(back.at[0, lax.rem(to + 32, 64)], ghost_in.at[1, owner_row], ghost_sem.at[1], 0, az=to).start()
+        ghost_in[1, pl.ds(owner_row, 1)] = back[0, pl.ds(opposite, 1)]
+
+    hand_out(peers[:32])
+    pl.when(leads_up)(lambda: hand_up(places[:32]))
+    pl.when(leads_down)(lambda: hand_down(places[:32]))
+    hand_out(peers[32:])
+    pl.when(leads_up)(lambda: hand_up(places[32:]))
+    pl.when(leads_down)(lambda: hand_down(places[32:]))
+    pl.when(leads_ghost)(hand_ghost)
+    ret[0, pl.ds(me, 1)] = back[0, pl.ds(me, 1)]
     stage(first, az_out, 5)
     az = along_az(az_out, az_in.at[1], az_sem.at[1])
     start_all(az)
@@ -736,20 +765,15 @@
     packed = pack_state(padded)
     for r in range(4):
         near_outer[1, 8 * r : 8 * r + 8, :] = packed[32 * r + 16 : 32 * r + 24]
-    arrived(ret.at[0], come_sem.at[0, 1])
-
-    rows = along_ax(ret.at[0, pl.ds(16, 48)], near2_low, ret.at[0, pl.ds(0, 48)], near2_high, near_sem)
-    start_ax(rows)
-    for r in range(4):
-        ghost_out[1, r] = ret[0, 16 * r]
-    ghost = copy(ghost_out.at[1], ghost_in.at[1], ghost_sem.at[1], 0, az=opposite)
-    ghost.start()
+    arrived(ret.at[0], come_sem.at[1, 0])
+
 
     def own_first(r):
         return packed_rows(ret.at[0], 16 * r, 16)
 
     near_azimuthal(own_first, own_marks, 1, near_rate)
-    came_ax(rows)
+    when_down(pltpu.make_async_copy(near2_low, near2_low, near_sem.at[1, 0]).wait)
+    when_up(pltpu.make_async_copy(near2_high, near2_high, near_sem.at[1, 1]).wait)
 
     def low_rim_two():
         for k in range(3):
@@ -761,7 +785,14 @@
 
     pl.when(row == 0)(low_rim_two)
     pl.when(row == 3)(high_rim_two)
-    ghost.wait_recv()
+    mirrored, ghost_arrived = ghost_in.at[1], ghost_sem.at[1, 1, 0]
+
+    def ghost_but_own():
+        part = mirrored.at[pl.ds(0, 3)]
+        pltpu.make_async_copy(part, part, ghost_arrived).wait()
+
+    pl.when(leads_ghost)(ghost_but_own)
+    pl.when(jnp.logical_not(leads_ghost))(pltpu.make_async_copy(mirrored, mirrored, ghost_arrived).wait)
 
     def near_second(r, slope, valid):
         value = own_state(r) * 0.75 + (own_first(r) + slope * time_step) * 0.25
@@ -789,12 +820,12 @@
         for v in range(5):
             first[v, r] = jnp.where(inner40, block(v, r)[3:43], first[v, r])
     came_all(az)
-    sent_all(az + [ghost])
+    sent_all(az)
     fill_az(1)
     azimuthal(padded, padded_flags, 1, rate)
     arrived(recv.at[1], go_sem.at[1, 1])
     project(recv.at[1], back.at[1], me, fwd, inv, twiddle, mix_high, mix_low)
-    spread(back.at[1], ret.at[1], me, peers, come_sem.at[1, 0], come_sem.at[1, 1])
+    spread(back.at[1], ret.at[1], me, peers, come_sem.at[0, 1], come_sem.at[1, 1])
     came_ax(ax2)
     rims(first, 1)
 
@@ -802,16 +833,22 @@
         second[v, r, rows, :] = state[v, r, rows, :] * 0.75 + (here + slope * time_step) * 0.25
 
     finish(first, low.at[1], high.at[1], flags, flow, fhigh, 1, rate, combine_second)
-    sent_ax(rows)
     for section in range(2):
         arrived(send.at[section], go_sem.at[section, 0])
     arrived(back.at[0], come_sem.at[0, 0])
+
+    def whole(buffer, s):
+        return pltpu.make_async_copy(buffer, buffer, s)
+
+    pl.when(leads_up)(whole(back.at[0], near_sem.at[0, 0]).wait)
+    pl.when(leads_down)(whole(back.at[0], near_sem.at[0, 1]).wait)
+    pl.when(leads_ghost)(lambda: arrived(back.at[0], ghost_sem.at[1, 0, 0]))
     arrived(ret.at[1], come_sem.at[1, 1])
     block = unpack(ret.at[1])
     for r in range(4):
         for v in range(5):
             out[v, r] = jnp.where(inner40, block(v, r)[3:43], second[v, r])
-    arrived(back.at[1], come_sem.at[1, 0])
+    arrived(back.at[1], come_sem.at[0, 1])
 
 
 def local(state, shock_flags):

time: 49.1 us -> 47.3 us (0.963)
  Pallas kernels: 48.2 us -> 46.4 us
    pallas_call x1, Pallas kernels: 48.2 us -> 46.4 us  [local(): pl.pallas_call(kernel, out_shape=jax.ShapeDtypeStruct(state.shape, f32),...]
where the time goes in v4:
time: 47.3 us; the launch traced here: 47.2 us
  Pallas kernels  46.4 us (98%)
  other arithmetic  0.8 us (2%)
    pallas_call x1, Pallas kernels, local(): pl.pallas_call(kernel, out_shape=jax.ShapeDtypeStruct(state.shape, f32),...  46.4 us

profile of v4, /device:TPU:1, one launch (start us, length us, event | category | flops | bytes accessed | tf_op | source)
XLA Modules:
  0.0 47.2 jit_solution(15890823642281107580)
XLA Ops:
  0.0 0.0 copy-start
  0.0 46.4 %shard_map.64 = f32[5,4,40,128]{3,2,1,0:T(8,128)S(1)} custom-call(f32[5,4,40,128]{3,2,1,0:T(8,128)} %state_hbm.1, s32[2,4,40,128]{3,2,1,0:T(8,128)} %flags_hbm.1, bf16[2,80,64]{2,1,0:T(8,128)(2,1)} %constant.20.fwd_hbm, bf16[2,64,80]{2,1,0:T(8,128)(2,1)} %constant.27.inv_hbm, f32[4,40,256]{2,1,0:T(8,128)} %constant.10.clone.twiddle_hbm, ...), custom_call_target="tpu_custom_call" | custom-call | tf_op jit(solution)/shard_map/pallas_call | solution.py:862
  46.4 0.0 copy-done
  46.4 0.8 %sub.11 = f32[5,4,40,128]{3,2,1,0:T(8,128)} subtract(f32[5,4,40,128]{3,2,1,0:T(8,128)S(1)} %shard_map.64, f32[5,4,40,128]{3,2,1,0:T(8,128)S(1)} %copy-done) | non-fusion elementwise | flops 102400 | bytes 1228800 | tf_op jit(solution)/shard_map/sub | solution.py:927
Async XLA Ops:
  0.0 46.4 %copy-start = (f32[5,4,40,128]{3,2,1,0:T(8,128)S(1)}, f32[5,4,40,128]{3,2,1,0:T(8,128)}, u32[]{:S(2)}) copy-start(f32[5,4,40,128]{3,2,1,0:T(8,128)} %state_hbm.1) | copy-start | bytes 1228804

commit v5 on v3

--- a/solution.py
+++ b/solution.py
@@ -162,10 +162,14 @@
     return jnp.maximum(a, b)
 
 
-def window(flags):
+def peak(flags):
     pair = largest(flags, at(flags, 1))
     four = largest(pair, at(pair, 2))
-    six = at(largest(four, at(pair, 4)), -2)
+    return at(largest(four, at(pair, 4)), -2)
+
+
+def window(flags):
+    six = peak(flags)
     return six.map(lambda a: a > 0.5) if isinstance(six, Rows) else six > 0.5
 
 
@@ -388,16 +392,103 @@
 
 
 def packed_rows(ref, first, count):
-    return jnp.concatenate([ref[first : first + count, 0, :], ref[first : first + count, 1, :]], axis=1)
-
-
-def unpack(ret):
-    lines = jnp.concatenate([packed_rows(ret, 0, 64), jnp.zeros((64, 256), jnp.float32)], axis=0)
-    turned = jnp.transpose(lines)
-
-    def block(v, r):
-        rows = turned[48 * v : 48 * v + 48]
-        return pltpu.roll(rows, 128 - 16 * r, 1) if r else rows
+    rows = pl.ds(first, count)
+    return jnp.concatenate([ref[rows, 0, :], ref[rows, 1, :]], axis=1)
+
+
+def place_of(r, group):
+    return 32 * (r % 2) + 8 * (r // 2 + 2 * group)
+
+
+def build_selectors(apart, copies):
+    to, source = lanes((256, 640)), lax.broadcasted_iota(jnp.int32, (256, 640), 0)
+    cell = lax.rem(to, 128)
+    hit = (cell < 48) & (source == cell + 48 * (to // 128))
+    apart[...] = jnp.where(hit, 1.0, 0.0).astype(jnp.bfloat16)
+    to, source = lanes((128, 256)), lax.broadcasted_iota(jnp.int32, (128, 256), 0)
+    hit = (source == lax.rem(to, 48)) & (to < 240)
+    copies[...] = jnp.where(hit, 1.0, 0.0).astype(jnp.bfloat16)
+
+
+def select(values, selector):
+    high, low = split(values)
+    both = dot(jnp.concatenate([high, low], axis=0), selector)
+    n = values.shape[0]
+    return both[:n] + both[n:]
+
+
+def line_rates(own_line, lines, extra, cycle, target, apart, copies):
+    lane = lanes((16, 256))
+    cell = lax.rem(lane, 48)
+    valid = (cell >= 3) & (cell < 43) & (lane < 240)
+    radius_here = jnp.full((16, 256), cycle, jnp.int32).astype(jnp.float32) + 0.5
+    inv_r = 1.0 / radius_here
+    inv_rh = 1.0 / (radius_here * (2.0 * math.pi / 2560))
+
+    def chunk(c):
+        first = c * 16
+        own = packed_rows(own_line, first, 16)
+        blocks = [packed_rows(lines.at[k], first, 16) for k in range(3)] + [own]
+        blocks += [packed_rows(lines.at[k], first, 16) for k in range(3, 6)]
+        blocks += [packed_rows(lines.at[k], first, 16) for k in (6, 7)]
+        apart_parts = select(jnp.concatenate(blocks, axis=0), apart[...])
+        parts = [apart_parts[:, 128 * k : 128 * k + 128] for k in range(5)]
+        inv_rho = inverse(jnp.where(parts[0] == 0.0, 1.0, parts[0]))
+        p = pressure(parts, inv_rho)
+        q_x, q_r, q_t = [parts[k] * inv_rho for k in (1, 2, 3)]
+        stacked = jnp.concatenate([p, q_x[:112], q_r[48:64], q_r[112:], q_t[48:64]], axis=0)
+        spread_out = select(stacked, copies[...])
+        wide = [spread_out[16 * k : 16 * k + 16] for k in range(20)]
+        wide_p = wide[:9]
+        f = [packed_flux(blocks[k], wide[9 + k], wide_p[k], 0) for k in range(7)]
+        q_r, q_t = wide[16], wide[19]
+        g = packed_flux(own, q_r, wide_p[3], 1)
+        turn = packed_flux(own, q_t, wide_p[3], 2)
+        drag = jnp.where(
+            slot((16, 256), 2),
+            pltpu.roll(own, 256 - 48, 1) * q_t + wide_p[3],
+            jnp.where(slot((16, 256), 3), -pltpu.roll(own, 48, 1) * q_t, 0.0),
+        )
+        sides = [packed_flux(blocks[7 + k], wide[17 + k], wide_p[7 + k], 1) for k in range(2)]
+        blocks = blocks[:7]
+        rows = pl.ds(first, 16)
+        marks = jnp.concatenate([extra[rows, 2, :], extra[rows, 3, :]], axis=1)
+        marks = [marks, pltpu.roll(marks, 256 - 48, 1), pltpu.roll(marks, 256 - 96, 1)]
+        marks = jnp.concatenate([m[:, :128] for m in marks], axis=0).astype(jnp.bfloat16)
+        marks = dot(marks, copies[...]) > 0.5
+        below, above, around = marks[:16], marks[16:32], marks[32:]
+        halves = []
+        for h in range(2):
+            pair = []
+            for w in range(2):
+                part = (slice(8 * h, 8 * h + 8), slice(128 * w, 128 * w + 128))
+                face = faces(
+                    Rows([x[part] for x in f]),
+                    Rows([x[part] for x in blocks]),
+                    Rows([None, None, below[part], above[part], None, None, None]),
+                    pick,
+                ).cells
+                pair.append(face[2] - face[3])
+            halves.append(jnp.concatenate(pair, axis=1))
+        face = faces(turn, own, around, pick)
+        slope = jnp.concatenate(halves, axis=0) + (at(face, -1) - face) * inv_rh
+        slope = slope - ((sides[1] - sides[0]) * 0.5 + (g - drag) * inv_r)
+        before = jnp.concatenate([extra[rows, 0, :], extra[rows, 1, :]], axis=1)
+        value = jnp.where(valid, before * 0.75 + (own + slope * time_step) * 0.25, 0.0)
+        target[rows, 0, :] = value[:, :128]
+        target[rows, 1, :] = value[:, 128:]
+
+    for c in range(4):
+        chunk(c)
+
+
+def unpack(rows):
+    n = rows.shape[0]
+    turned = jnp.transpose(jnp.concatenate([rows, jnp.zeros((128 - n, 256), jnp.float32)], axis=0))
+
+    def block(v, k):
+        cells = turned[48 * v : 48 * v + 48]
+        return pltpu.roll(cells, (128 - k) % 128, 1) if k % 128 else cells
 
     return block
 
@@ -475,22 +566,24 @@
     state, flags, fwd, inv, twiddle, mine, mix_high, mix_low, padded, padded_flags, rate, first, second,
     az_out, az_in, azf_out, azf_in, low, high, flow, fhigh,
     near, near_rate, near_low, near_high, near_outer, ends_out, ends_in, marks, marks_low, marks_high,
-    mark_ends_out, mark_ends_in, ghost_out, ghost_in, near2_low, near2_high,
-    send, recv, back, ret,
-    sem, az_sem, azf_sem, ax_sem, axf_sem, end_sem, mark_end_sem, row_sem, mark_row_sem, ghost_sem, near_sem,
-    go_sem, come_sem,
+    mark_ends_out, mark_ends_in, ghost_out, ghost_in,
+    send, recv, back, ret, lines, extra_out, extra_in, outer_out, rim_in, apart, copies,
+    sem, az_sem, azf_sem, ax_sem, axf_sem, end_sem, mark_end_sem, row_sem, mark_row_sem, ghost_sem,
+    go_sem, come_sem, line_sem, extra_sem, outer_sem, rim_sem,
 ):
     me, row = lax.axis_index("az"), lax.axis_index("ax")
     right, left = lax.rem(me + 1, 64), lax.rem(me + 63, 64)
     upper, lower = lax.rem(row + 1, 4), lax.rem(row + 3, 4)
     opposite = lax.rem(me + 32, 64)
+    z, x, y = lax.rem(me, 8), lax.rem(me // 8, 4), me // 32
+    level, cycle = y + 2 * lax.rem(x, 2), 8 * (x // 2) + z
     pairs = [
         (state_hbm, state),
         (flags_hbm, flags),
         (fwd_hbm, fwd),
         (inv_hbm, inv),
         (twiddle_hbm, twiddle),
-        (band.at[lax.rem(me, 16)], mine),
+        (band.at[cycle], mine),
     ]
     loads = [pltpu.make_async_copy(a, b, sem.at[k]) for k, (a, b) in enumerate(pairs)]
     for item in loads:
@@ -605,6 +698,7 @@
     for item in loads[2:]:
         item.wait()
     build_mix(mine, mix_high, mix_low)
+    build_selectors(apart, copies)
 
     came_all(ends)
     came_all(mark_ends)
@@ -649,8 +743,11 @@
         return lambda r: near_outer[section, 8 * r : 8 * r + 8, :]
 
     def hand_in(section, r, value):
-        send[section, 16 * r : 16 * r + 16, 0, :] = value[:, :128]
-        send[section, 16 * r : 16 * r + 16, 1, :] = value[:, 128:]
+        for group in range(2):
+            first_place = place_of(r, group)
+            for h in range(2):
+                part = value[8 * group : 8 * group + 8, 128 * h : 128 * h + 128]
+                send[section, first_place : first_place + 8, h, :] = part
 
     def near_first(r, slope, valid):
         hand_in(0, r, jnp.where(valid, own_state(r) + slope * time_step, 0.0))
@@ -668,6 +765,20 @@
     )
     spread(send.at[0], recv.at[0], me, peers, go_sem.at[0, 0], go_sem.at[0, 1])
 
+    tall = Rows(mark_list()).map(lambda a: replicate(pltpu.roll(a, 80, 1)))
+    axial_marks = peak(tall).cells
+    for r in range(4):
+        low_part, high_part, turn_part = axial_marks[2 + r], axial_marks[3 + r], peak(tall.cells[3 + r])
+        own_slot = [slot((16, 256), k) for k in range(3)]
+        row_marks = jnp.where(own_slot[1], high_part, jnp.where(own_slot[2], turn_part, 0.0))
+        row_marks = jnp.where(own_slot[0], low_part, row_marks)
+        whole_row = [own_state(r)[:, :128], own_state(r)[:, 128:], row_marks[:, :128], row_marks[:, 128:]]
+        for group in range(2):
+            first_place = place_of(r, group)
+            for k in range(4):
+                extra_out[first_place : first_place + 8, k, :] = whole_row[k][8 * group : 8 * group + 8]
+    spread(extra_out, extra_in, me, peers, extra_sem.at[0], extra_sem.at[1])
+
     sent_ax(rows)
     sent_ax(mark_rows)
     sent_all(ends + mark_ends + [ghost])
@@ -722,96 +833,137 @@
 
     finish(state, low.at[0], high.at[0], flags, flow, fhigh, 0, rate, combine_first)
     sent_all(az + azf)
-    arrived(recv.at[0], go_sem.at[0, 1])
-    project(recv.at[0], back.at[0], me, fwd, inv, twiddle, mix_high, mix_low)
-    spread(back.at[0], ret.at[0], me, peers, come_sem.at[0, 0], come_sem.at[0, 1])
-    stage(first, az_out, 5)
-    az = along_az(az_out, az_in.at[1], az_sem.at[1])
-    start_all(az)
-    ax2 = wide_ax(first, low.at[1], high.at[1], ax_sem.at[1])
-    start_ax(ax2)
     for v in range(5):
         for r in range(4):
             padded[v, r, 3:43] = first[v, r]
     packed = pack_state(padded)
     for r in range(4):
-        near_outer[1, 8 * r : 8 * r + 8, :] = packed[32 * r + 16 : 32 * r + 24]
-    arrived(ret.at[0], come_sem.at[0, 1])
-
-    rows = along_ax(ret.at[0, pl.ds(16, 48)], near2_low, ret.at[0, pl.ds(0, 48)], near2_high, near_sem)
-    start_ax(rows)
-    for r in range(4):
-        ghost_out[1, r] = ret[0, 16 * r]
-    ghost = copy(ghost_out.at[1], ghost_in.at[1], ghost_sem.at[1], 0, az=opposite)
-    ghost.start()
-
-    def own_first(r):
-        return packed_rows(ret.at[0], 16 * r, 16)
-
-    near_azimuthal(own_first, own_marks, 1, near_rate)
-    came_ax(rows)
-
-    def low_rim_two():
-        for k in range(3):
-            near2_low[16 * k : 16 * k + 16] = ret[0, 0:16]
-
-    def high_rim_two():
-        for k in range(3):
-            near2_high[16 * k : 16 * k + 16] = ret[0, 48:64]
-
-    pl.when(row == 0)(low_rim_two)
-    pl.when(row == 3)(high_rim_two)
-    ghost.wait_recv()
-
-    def near_second(r, slope, valid):
-        value = own_state(r) * 0.75 + (own_first(r) + slope * time_step) * 0.25
-        hand_in(1, r, jnp.where(valid, value, 0.0))
-
-    near_finish(
-        lambda k: packed_rows(near2_low, 16 * k, 16),
-        own_first,
-        lambda k: packed_rows(near2_high, 16 * k, 16),
-        outer_rows(1),
-        ghost_row(1),
-        mark_list(),
-        1,
-        near_rate,
-        near_second,
-    )
-    spread(send.at[1], recv.at[1], me, peers, go_sem.at[1, 0], go_sem.at[1, 1])
-
-    inner40 = lanes((40, 128)) < NRING
+        outer_out[r, 0:1, :] = packed[32 * r + 16 : 32 * r + 17, :128]
+        outer_out[r, 1:2, :] = packed[32 * r + 16 : 32 * r + 17, 128:]
+    for r in range(4):
+        last = place_of(r, 1) + 7
+        beyond = copy(outer_out.at[r], lines.at[7, me], outer_sem, 0, az=last)
+        pl.when(me != last)(beyond.start)
+    is_last, is_first = cycle == 15, cycle == 0
+
+    def keep_outer():
+        lines[7, pl.ds(me, 1)] = outer_out[pl.ds(level, 1)]
+
+    pl.when(is_last)(keep_outer)
+    stage(first, az_out, 5)
+    az = along_az(az_out, az_in.at[1], az_sem.at[1])
+    start_all(az)
+    arrived(recv.at[0], go_sem.at[0, 1])
+    project(recv.at[0], back.at[0], me, fwd, inv, twiddle, mix_high, mix_low)
+
+    column = 16 * (x // 2) + z
+    meets = []
+    for step in range(1, 4):
+        over, under = level + step, level + 4 - step
+        to_row, to_level = row + over // 4, lax.rem(over, 4)
+        to = 32 * lax.rem(to_level, 2) + 8 * (to_level // 2) + column
+        item = copy(back.at[0], lines.at[3 - step], line_sem, 3 - step, ax=to_row, az=to)
+        has_over, has_under = (row < 3) | (over < 4), (row > 0) | (under >= 4)
+        meets.append((item, has_over, has_under))
+        to_row, to_level = row - 1 + under // 4, lax.rem(under, 4)
+        to = 32 * lax.rem(to_level, 2) + 8 * (to_level // 2) + column
+        item = copy(back.at[0], lines.at[2 + step], line_sem, 2 + step, ax=to_row, az=to)
+        meets.append((item, has_under, has_over))
+    base = 32 * lax.rem(level, 2) + 8 * (level // 2)
+    ahead, behind = cycle + 1, cycle + 15
+    to = base + 16 * (ahead // 8) + lax.rem(ahead, 8)
+    item = copy(back.at[0], lines.at[6], line_sem, 6, az=to)
+    not_first, not_last = jnp.logical_not(is_first), jnp.logical_not(is_last)
+    meets.append((item, not_last, not_first))
+    behind = lax.rem(behind, 16)
+    to = base + 16 * (behind // 8) + lax.rem(behind, 8)
+    item = copy(back.at[0], lines.at[7], line_sem, 7, az=to)
+    meets.append((item, not_first, not_last))
+    for item, sends, _ in meets:
+        pl.when(sends)(item.start)
+
+    def hand_rim():
+        for to in peers:
+            copy(back.at[0, to], rim_in.at[level], rim_sem, 0, az=to).start()
+        rim_in[pl.ds(level, 1)] = back[0, pl.ds(me, 1)]
+
+    pl.when(is_last)(hand_rim)
+
+    def mirror():
+        lane = lanes((64, 128))
+        for h in range(2):
+            flipped = (lane + 128 * h >= 96) & (lane + 128 * h < 192)
+            turned = jnp.concatenate([back[0, 32:64, h, :], back[0, 0:32, h, :]], axis=0)
+            lines[6, :, h, :] = jnp.where(flipped, -turned, turned)
+
+    pl.when(is_first)(mirror)
+    arrived(extra_in, extra_sem.at[1])
+    for item, _, comes in meets:
+        pl.when(comes)(item.wait_recv)
+    pl.when(is_last)(lambda: arrived(lines.at[7], outer_sem.at[1, 0]))
+    for r in range(3):
+
+        def clamp_low():
+            for step in range(r + 1, 4):
+                lines[3 - step] = lines[3 - r] if r else back[0]
+
+        def clamp_high():
+            for step in range(r + 1, 4):
+                lines[2 + step] = lines[2 + r] if r else back[0]
+
+        pl.when((row == 0) & (level == r))(clamp_low)
+        pl.when((row == 3) & (level == 3 - r))(clamp_high)
+    ax2 = wide_ax(first, low.at[1], high.at[1], ax_sem.at[1])
+    start_ax(ax2)
+    line_rates(back.at[0], lines, extra_in, cycle, recv.at[1], apart, copies)
+    project(recv.at[1], back.at[1], me, fwd, inv, twiddle, mix_high, mix_low)
+    spread(back.at[1], ret, me, peers, come_sem.at[0], come_sem.at[1])
+
     sent_ax(ax)
     sent_ax(axf)
-    sent_ax(ax2)
-    block = unpack(ret.at[0])
-    for r in range(4):
-        for v in range(5):
-            first[v, r] = jnp.where(inner40, block(v, r)[3:43], first[v, r])
     came_all(az)
-    sent_all(az + [ghost])
+    sent_all(az)
     fill_az(1)
     azimuthal(padded, padded_flags, 1, rate)
-    arrived(recv.at[1], go_sem.at[1, 1])
-    project(recv.at[1], back.at[1], me, fwd, inv, twiddle, mix_high, mix_low)
-    spread(back.at[1], ret.at[1], me, peers, come_sem.at[1, 0], come_sem.at[1, 1])
+    sent_ax(ax2)
     came_ax(ax2)
     rims(first, 1)
 
+    def rim_but_own():
+        part = rim_in.at[pl.ds(0, 3)]
+        pltpu.make_async_copy(part, part, rim_sem.at[1, 0]).wait()
+
+    pl.when(is_last)(rim_but_own)
+    pl.when(not_last)(pltpu.make_async_copy(rim_in, rim_in, rim_sem.at[1, 0]).wait)
+    block = unpack(jnp.concatenate([packed_rows(rim_in, 0, 4), jnp.zeros((4, 256), jnp.float32)], axis=0))
+    lane40 = lanes((40, 128))
+    for r in range(4):
+        for v in range(5):
+            first[v, r] = jnp.where(lane40 == 15, block(v, r - 15)[3:43], first[v, r])
+
     def combine_second(v, r, rows, here, slope):
         second[v, r, rows, :] = state[v, r, rows, :] * 0.75 + (here + slope * time_step) * 0.25
 
     finish(first, low.at[1], high.at[1], flags, flow, fhigh, 1, rate, combine_second)
-    sent_ax(rows)
-    for section in range(2):
-        arrived(send.at[section], go_sem.at[section, 0])
-    arrived(back.at[0], come_sem.at[0, 0])
-    arrived(ret.at[1], come_sem.at[1, 1])
-    block = unpack(ret.at[1])
+    arrived(send.at[0], go_sem.at[0, 0])
+    arrived(extra_out, extra_sem.at[0])
+    for item, sends, _ in meets:
+        pl.when(sends)(item.wait_send)
+    pl.when(is_last)(lambda: arrived(back.at[0], rim_sem.at[0, 0]))
+
+    def outers(n):
+        part = outer_out.at[pl.ds(0, n)]
+        pltpu.make_async_copy(part, part, outer_sem.at[0, 0]).wait()
+
+    pl.when(is_last)(lambda: outers(3))
+    pl.when(not_last)(lambda: outers(4))
+    arrived(ret, come_sem.at[1])
+    order = [packed_rows(ret, place_of(r, group), 8) for r in range(4) for group in range(2)]
+    block = unpack(jnp.concatenate(order, axis=0))
     for r in range(4):
         for v in range(5):
-            out[v, r] = jnp.where(inner40, block(v, r)[3:43], second[v, r])
-    arrived(back.at[1], come_sem.at[1, 0])
+            out[v, r] = jnp.where(lane40 < NRING, block(v, 16 * r)[3:43], second[v, r])
+    arrived(back.at[1], come_sem.at[0])
 
 
 def local(state, shock_flags):
@@ -863,12 +1015,17 @@
             pltpu.VMEM((2, 16, 128), f32),
             pltpu.VMEM((2, 4, 2, 128), f32),
             pltpu.VMEM((2, 4, 2, 128), f32),
-            pltpu.VMEM((48, 2, 128), f32),
-            pltpu.VMEM((48, 2, 128), f32),
+            pltpu.VMEM((1, 64, 2, 128), f32),
             pltpu.VMEM((2, 64, 2, 128), f32),
             pltpu.VMEM((2, 64, 2, 128), f32),
-            pltpu.VMEM((2, 64, 2, 128), f32),
-            pltpu.VMEM((2, 64, 2, 128), f32),
+            pltpu.VMEM((64, 2, 128), f32),
+            pltpu.VMEM((8, 64, 2, 128), f32),
+            pltpu.VMEM((64, 4, 128), f32),
+            pltpu.VMEM((64, 4, 128), f32),
+            pltpu.VMEM((4, 2, 128), f32),
+            pltpu.VMEM((4, 2, 128), f32),
+            pltpu.VMEM((256, 640), jnp.bfloat16),
+            pltpu.VMEM((128, 256), jnp.bfloat16),
             dma((6,)),
             dma((2, 2, 2)),
             dma((2, 2)),
@@ -879,9 +1036,12 @@
             dma((2, 2)),
             dma((2, 2)),
             dma((2, 2, 1)),
-            dma((2, 2)),
-            dma((2, 2)),
-            dma((2, 2)),
+            dma((1, 2)),
+            dma((2,)),
+            dma((2, 8)),
+            dma((2,)),
+            dma((2, 1)),
+            dma((2, 1)),
         ],
         compiler_params=pltpu.CompilerParams(
             collective_id=0, has_side_effects=True, vmem_limit_bytes=40 * 1024 * 1024

time: 49.1 us -> 44.5 us (0.906)
  Pallas kernels: 48.2 us -> 43.2 us
    pallas_call x1, Pallas kernels: 48.2 us -> 43.2 us  [local(): pl.pallas_call(kernel, out_shape=jax.ShapeDtypeStruct(state.shape, f32),...]
where the time goes in v5:
time: 44.5 us; the launch traced here: 44 us
  Pallas kernels  43.2 us (97%)
  other arithmetic  0.8 us (2%)
    pallas_call x1, Pallas kernels, local(): pl.pallas_call(kernel, out_shape=jax.ShapeDtypeStruct(state.shape, f32),...  43.2 us

profile of v5, /device:TPU:1, one launch (start us, length us, event | category | flops | bytes accessed | tf_op | source)
XLA Modules:
  0.0 44.0 jit_solution(17665335813472230770)
XLA Ops:
  0.0 0.0 copy-start
  0.0 43.2 %shard_map.64 = f32[5,4,40,128]{3,2,1,0:T(8,128)S(1)} custom-call(f32[5,4,40,128]{3,2,1,0:T(8,128)} %state_hbm.1, s32[2,4,40,128]{3,2,1,0:T(8,128)} %flags_hbm.1, bf16[2,80,64]{2,1,0:T(8,128)(2,1)} %constant.20.fwd_hbm, bf16[2,64,80]{2,1,0:T(8,128)(2,1)} %constant.27.inv_hbm, f32[4,40,256]{2,1,0:T(8,128)} %constant.10.clone.twiddle_hbm, ...), custom_call_target="tpu_custom_call" | custom-call | tf_op jit(solution)/shard_map/pallas_call | solution.py:977
  43.2 0.0 copy-done
  43.2 0.8 %sub.11 = f32[5,4,40,128]{3,2,1,0:T(8,128)} subtract(f32[5,4,40,128]{3,2,1,0:T(8,128)S(1)} %shard_map.64, f32[5,4,40,128]{3,2,1,0:T(8,128)S(1)} %copy-done) | non-fusion elementwise | flops 102400 | bytes 1228800 | tf_op jit(solution)/shard_map/sub | solution.py:1050
Async XLA Ops:
  0.0 43.2 %copy-start = (f32[5,4,40,128]{3,2,1,0:T(8,128)S(1)}, f32[5,4,40,128]{3,2,1,0:T(8,128)}, u32[]{:S(2)}) copy-start(f32[5,4,40,128]{3,2,1,0:T(8,128)} %state_hbm.1) | copy-start | bytes 1228804

commit v6 on v5

--- a/solution.py
+++ b/solution.py
@@ -202,16 +202,36 @@
         switch = window(flags[section, r])
         for v in range(5):
             face = faces(f[v], u[v], switch, pick)
-            rate[v, r] = (at(face, 3)[:40] - at(face, 2)[:40]) * scale
+            rate[v, r] = rate[v, r] + (at(face, 3)[:40] - at(face, 2)[:40]) * scale
         return carry
 
     lax.fori_loop(0, 4, row, 0)
 
 
-def finish(own, low, high, flags, flags_low, flags_high, section, rate, combine):
+def radial_terms(own, rate):
     inv_r = 1.0 / radius(8)
     lane = lanes((8, 128))
 
+    def chunk(c, carry):
+        at8 = pl.ds(pl.multiple_of(c * 8, 8), 8)
+        for r in range(4):
+            here = [own[v, r, at8, :] for v in range(5)]
+            inv_here = inverse(here[0])
+            p_here = pressure(here, inv_here)
+            g = fluxes(here, here[2] * inv_here, p_here, 1)
+            swirl = here[3] * inv_here
+            extra = [None, None, here[3] * swirl + p_here, -here[2] * swirl, None]
+            for v in range(5):
+                before = pltpu.roll(g[v], 1, 1)
+                after = jnp.where(lane == 127, g[v], pltpu.roll(g[v], 127, 1))
+                away = g[v] if extra[v] is None else g[v] - extra[v]
+                rate[v, r, at8, :] = (before - after) * 0.5 - away * inv_r
+        return carry
+
+    lax.fori_loop(0, 5, chunk, 0)
+
+
+def finish(own, low, high, flags, flags_low, flags_high, section, rate, combine):
     def chunk(c, carry):
         at8 = pl.ds(pl.multiple_of(c * 8, 8), 8)
         u = [
@@ -229,26 +249,11 @@
         ).map(lambda a: a.astype(jnp.float32))
         switch = window(marks)
         inv_rho = u[0].map(inverse)
-        p = pressure(u, inv_rho)
-        f = fluxes(u, u[1] * inv_rho, p, 0)
-        radial, source = [], []
-        for r in range(4):
-            here = [u[v].cells[3 + r] for v in range(5)]
-            inv_here, p_here = inv_rho.cells[3 + r], p.cells[3 + r]
-            g = fluxes(here, here[2] * inv_here, p_here, 1)
-            swirl = here[3] * inv_here
-            extra = [None, None, here[3] * swirl + p_here, -here[2] * swirl, None]
-            terms = []
-            for v in range(5):
-                before = pltpu.roll(g[v], 1, 1)
-                after = jnp.where(lane == 127, g[v], pltpu.roll(g[v], 127, 1))
-                away = g[v] if extra[v] is None else g[v] - extra[v]
-                terms.append((after - before) * 0.5 + away * inv_r)
-            radial.append(terms)
+        f = fluxes(u, u[1] * inv_rho, pressure(u, inv_rho), 0)
         for v in range(5):
             face = faces(f[v], u[v], switch, pick).cells
             for r in range(4):
-                slope = rate[v, r, at8, :] - (face[3 + r] - face[2 + r]) - radial[r][v]
+                slope = rate[v, r, at8, :] - (face[3 + r] - face[2 + r])
                 combine(v, r, at8, u[v].cells[3 + r], slope)
         return carry
 
@@ -311,12 +316,6 @@
     return four + pltpu.roll(one, 192, 1)
 
 
-def primitives(u):
-    parts = [u[:, :128]] + [pltpu.roll(u, 256 - 48 * k, 1)[:, :128] for k in range(1, 5)]
-    inv_rho = inverse(parts[0])
-    return parts, inv_rho, pressure(parts, inv_rho)
-
-
 def slot(shape, k):
     lane = lanes(shape)
     return (lane >= 48 * k) & (lane < 48 * k + 48)
@@ -327,49 +326,48 @@
     return u * q + jnp.where(own, p, jnp.where(energy, p * q, 0.0))
 
 
-def near_azimuthal(own, marks, section, rate):
-    for r in range(4):
-        u = own(r)
-        parts, inv_rho, p = primitives(u)
-        q = replicate(parts[3] * inv_rho)
-        f = packed_flux(u, q, replicate(p), 2)
-        mark = marks(r)
-        switch = window(replicate(pltpu.roll(mark, 80, 1) if section else mark))
-        face = faces(f, u, switch, pick)
-        cycle = lax.broadcasted_iota(jnp.int32, (16, 256), 0).astype(jnp.float32) + 0.5
-        rate[16 * r : 16 * r + 16, :] = (at(face, -1) - face) * (1.0 / (cycle * (2.0 * math.pi / 2560)))
-
-
-def near_finish(low, own, high, outer, ghost, marks, section, rate, combine):
+def near_azimuthal(own, marks, rate, apart, copies):
+    blocks = [own(r) for r in range(4)]
+    (_, _, q_t), p = stacked_primitives(blocks, apart)
+    wide = select(jnp.concatenate([p, q_t], axis=0), copies[...])
+    every = dot(jnp.concatenate([marks(r) for r in range(4)], axis=0).astype(jnp.bfloat16), copies[...])
+    cycle = lax.broadcasted_iota(jnp.int32, (16, 256), 0).astype(jnp.float32) + 0.5
+    inv_rh = 1.0 / (cycle * (2.0 * math.pi / 2560))
+    for r, u in enumerate(blocks):
+        wide_p, wide_t = wide[16 * r : 16 * r + 16], wide[64 + 16 * r : 80 + 16 * r]
+        f = packed_flux(u, wide_t, wide_p, 2)
+        face = faces(f, u, window(every[16 * r : 16 * r + 16]), pick)
+        rate[16 * r : 16 * r + 16, :] = (at(face, -1) - face) * inv_rh
+
+
+def near_finish(low, own, high, outer, ghost, marks, rate, apart, copies, combine):
     blocks = [low(k) for k in range(3)] + [own(r) for r in range(4)] + [high(k) for k in range(3)]
-    f, switches, radial = [], [], []
-    for k, u in enumerate(blocks):
-        parts, inv_rho, p = primitives(u)
-        wide_p = replicate(p)
-        f.append(packed_flux(u, replicate(parts[1] * inv_rho), wide_p, 0))
-        mark = marks[k]
-        switches.append(replicate(pltpu.roll(mark, 80, 1) if section else mark))
-        if 3 <= k < 7:
-            r = k - 3
-            beyond = outer(r)
-            row = lax.broadcasted_iota(jnp.int32, (8, 256), 0)
-            negated = slot((8, 256), 2) | slot((8, 256), 3)
-            mirror = jnp.broadcast_to(ghost(r), (8, 256))
-            mirror = jnp.where(negated, -mirror, mirror)
-            beyond = jnp.where(row == 7, mirror, beyond)
-            b_parts, b_inv, b_p = primitives(beyond)
-            g_beyond = packed_flux(beyond, replicate(b_parts[2] * b_inv), replicate(b_p), 1)
-            g = packed_flux(u, replicate(parts[2] * inv_rho), wide_p, 1)
-            q_t = replicate(parts[3] * inv_rho)
-            extra = jnp.where(
-                slot((16, 256), 2),
-                pltpu.roll(u, 256 - 48, 1) * q_t + wide_p,
-                jnp.where(slot((16, 256), 3), -pltpu.roll(u, 48, 1) * q_t, 0.0),
-            )
-            ring = jnp.concatenate([g, g_beyond], axis=0)
-            after, before = pltpu.roll(ring, 23, 0)[:16], pltpu.roll(ring, 1, 0)[:16]
-            cycle = lax.broadcasted_iota(jnp.int32, (16, 256), 0).astype(jnp.float32) + 0.5
-            radial.append((after - before) * 0.5 + (g - extra) * (1.0 / cycle))
+    row = lax.broadcasted_iota(jnp.int32, (8, 256), 0)
+    negated = slot((8, 256), 2) | slot((8, 256), 3)
+    beyond = []
+    for r in range(4):
+        mirrored = jnp.broadcast_to(ghost(r), (8, 256))
+        beyond.append(jnp.where(row == 7, jnp.where(negated, -mirrored, mirrored), outer(r)))
+    (q_x, q_r, q_t), p = stacked_primitives(blocks + beyond, apart)
+    stacked = jnp.concatenate([p, q_x[:160], q_r[48:112], q_r[160:], q_t[48:112]], axis=0)
+    wide = select(stacked, copies[...])
+    every = dot(jnp.concatenate(marks, axis=0).astype(jnp.bfloat16), copies[...])
+    switches = [every[16 * k : 16 * k + 16] for k in range(10)]
+    f = [
+        packed_flux(u, wide[192 + 16 * k : 208 + 16 * k], wide[16 * k : 16 * k + 16], 0)
+        for k, u in enumerate(blocks)
+    ]
+    cycle = lax.broadcasted_iota(jnp.int32, (16, 256), 0).astype(jnp.float32) + 0.5
+    inv_r = 1.0 / cycle
+    radial = []
+    for r in range(4):
+        u, wide_p = blocks[3 + r], wide[48 + 16 * r : 64 + 16 * r]
+        g = packed_flux(u, wide[352 + 16 * r : 368 + 16 * r], wide_p, 1)
+        g_beyond = packed_flux(beyond[r], wide[416 + 8 * r : 424 + 8 * r], wide[160 + 8 * r : 168 + 8 * r], 1)
+        drag = drag_of(u, wide[448 + 16 * r : 464 + 16 * r], wide_p)
+        ring = jnp.concatenate([g, g_beyond], axis=0)
+        after, before = pltpu.roll(ring, 23, 0)[:16], pltpu.roll(ring, 1, 0)[:16]
+        radial.append((after - before) * 0.5 + (g - drag) * inv_r)
     slopes = [[[None, None], [None, None]] for _ in range(4)]
     for h in range(2):
         for w in range(2):
@@ -397,7 +395,7 @@
 
 
 def place_of(r, group):
-    return 32 * (r % 2) + 8 * (r // 2 + 2 * group)
+    return 32 * group + 8 * r
 
 
 def build_selectors(apart, copies):
@@ -417,46 +415,58 @@
     return both[:n] + both[n:]
 
 
-def line_rates(own_line, lines, extra, cycle, target, apart, copies):
+def stacked_primitives(blocks, apart):
+    every = select(jnp.concatenate(blocks, axis=0), apart[...])
+    parts = [every[:, 128 * k : 128 * k + 128] for k in range(5)]
+    inv_rho = inverse(jnp.where(parts[0] == 0.0, 1.0, parts[0]))
+    return [parts[k] * inv_rho for k in (1, 2, 3)], pressure(parts, inv_rho)
+
+
+def drag_of(u, q_t, p):
+    turned = jnp.where(slot(u.shape, 3), -pltpu.roll(u, 48, 1) * q_t, 0.0)
+    return jnp.where(slot(u.shape, 2), pltpu.roll(u, 256 - 48, 1) * q_t + p, turned)
+
+
+def line_alone(own_line, extra, cycle, partial, apart, copies):
+    radius_here = jnp.full((16, 256), cycle, jnp.int32).astype(jnp.float32) + 0.5
+    inv_r = 1.0 / radius_here
+    inv_rh = 1.0 / (radius_here * (2.0 * math.pi / 2560))
+    blocks = [packed_rows(own_line, 16 * c, 16) for c in range(4)]
+    (_, q_r, q_t), p = stacked_primitives(blocks, apart)
+    wide = select(jnp.concatenate([p, q_r, q_t], axis=0), copies[...])
+    marks = jnp.concatenate([extra[:, 2, :], extra[:, 3, :]], axis=1)
+    marks = pltpu.roll(marks, 256 - 96, 1)[:, :128].astype(jnp.bfloat16)
+    marks = dot(marks, copies[...]) > 0.5
+    for c, own in enumerate(blocks):
+        wide_p, wide_r, wide_t = [wide[64 * k + 16 * c : 64 * k + 16 * c + 16] for k in range(3)]
+        g = packed_flux(own, wide_r, wide_p, 1)
+        turn = packed_flux(own, wide_t, wide_p, 2)
+        face = faces(turn, own, marks[16 * c : 16 * c + 16], pick)
+        slope = (at(face, -1) - face) * inv_rh - (g - drag_of(own, wide_t, wide_p)) * inv_r
+        partial[16 * c : 16 * c + 16, :] = slope
+
+
+def line_rates(own_line, lines, extra, partial, target, apart, copies):
     lane = lanes((16, 256))
     cell = lax.rem(lane, 48)
     valid = (cell >= 3) & (cell < 43) & (lane < 240)
-    radius_here = jnp.full((16, 256), cycle, jnp.int32).astype(jnp.float32) + 0.5
-    inv_r = 1.0 / radius_here
-    inv_rh = 1.0 / (radius_here * (2.0 * math.pi / 2560))
-
-    def chunk(c):
-        first = c * 16
+    for c in range(4):
+        first = 16 * c
         own = packed_rows(own_line, first, 16)
         blocks = [packed_rows(lines.at[k], first, 16) for k in range(3)] + [own]
-        blocks += [packed_rows(lines.at[k], first, 16) for k in range(3, 6)]
-        blocks += [packed_rows(lines.at[k], first, 16) for k in (6, 7)]
-        apart_parts = select(jnp.concatenate(blocks, axis=0), apart[...])
-        parts = [apart_parts[:, 128 * k : 128 * k + 128] for k in range(5)]
-        inv_rho = inverse(jnp.where(parts[0] == 0.0, 1.0, parts[0]))
-        p = pressure(parts, inv_rho)
-        q_x, q_r, q_t = [parts[k] * inv_rho for k in (1, 2, 3)]
-        stacked = jnp.concatenate([p, q_x[:112], q_r[48:64], q_r[112:], q_t[48:64]], axis=0)
+        blocks += [packed_rows(lines.at[k], first, 16) for k in range(3, 8)]
+        (q_x, q_r, _), p = stacked_primitives(blocks, apart)
+        stacked = jnp.concatenate([p, q_x[:112], q_r[112:]], axis=0)
         spread_out = select(stacked, copies[...])
-        wide = [spread_out[16 * k : 16 * k + 16] for k in range(20)]
-        wide_p = wide[:9]
-        f = [packed_flux(blocks[k], wide[9 + k], wide_p[k], 0) for k in range(7)]
-        q_r, q_t = wide[16], wide[19]
-        g = packed_flux(own, q_r, wide_p[3], 1)
-        turn = packed_flux(own, q_t, wide_p[3], 2)
-        drag = jnp.where(
-            slot((16, 256), 2),
-            pltpu.roll(own, 256 - 48, 1) * q_t + wide_p[3],
-            jnp.where(slot((16, 256), 3), -pltpu.roll(own, 48, 1) * q_t, 0.0),
-        )
-        sides = [packed_flux(blocks[7 + k], wide[17 + k], wide_p[7 + k], 1) for k in range(2)]
+        wide = [spread_out[16 * k : 16 * k + 16] for k in range(18)]
+        f = [packed_flux(blocks[k], wide[9 + k], wide[k], 0) for k in range(7)]
+        sides = [packed_flux(blocks[7 + k], wide[16 + k], wide[7 + k], 1) for k in range(2)]
         blocks = blocks[:7]
         rows = pl.ds(first, 16)
         marks = jnp.concatenate([extra[rows, 2, :], extra[rows, 3, :]], axis=1)
-        marks = [marks, pltpu.roll(marks, 256 - 48, 1), pltpu.roll(marks, 256 - 96, 1)]
-        marks = jnp.concatenate([m[:, :128] for m in marks], axis=0).astype(jnp.bfloat16)
-        marks = dot(marks, copies[...]) > 0.5
-        below, above, around = marks[:16], marks[16:32], marks[32:]
+        marks = jnp.concatenate([marks[:, :128], pltpu.roll(marks, 256 - 48, 1)[:, :128]], axis=0)
+        marks = dot(marks.astype(jnp.bfloat16), copies[...]) > 0.5
+        below, above = marks[:16], marks[16:]
         halves = []
         for h in range(2):
             pair = []
@@ -470,16 +480,11 @@
                 ).cells
                 pair.append(face[2] - face[3])
             halves.append(jnp.concatenate(pair, axis=1))
-        face = faces(turn, own, around, pick)
-        slope = jnp.concatenate(halves, axis=0) + (at(face, -1) - face) * inv_rh
-        slope = slope - ((sides[1] - sides[0]) * 0.5 + (g - drag) * inv_r)
+        slope = jnp.concatenate(halves, axis=0) + partial[rows, :] - (sides[1] - sides[0]) * 0.5
         before = jnp.concatenate([extra[rows, 0, :], extra[rows, 1, :]], axis=1)
         value = jnp.where(valid, before * 0.75 + (own + slope * time_step) * 0.25, 0.0)
         target[rows, 0, :] = value[:, :128]
         target[rows, 1, :] = value[:, 128:]
-
-    for c in range(4):
-        chunk(c)
 
 
 def unpack(rows):
@@ -576,7 +581,7 @@
     upper, lower = lax.rem(row + 1, 4), lax.rem(row + 3, 4)
     opposite = lax.rem(me + 32, 64)
     z, x, y = lax.rem(me, 8), lax.rem(me // 8, 4), me // 32
-    level, cycle = y + 2 * lax.rem(x, 2), 8 * (x // 2) + z
+    level, cycle = x, 8 * y + z
     pairs = [
         (state_hbm, state),
         (flags_hbm, flags),
@@ -685,6 +690,7 @@
     azf = along_az(azf_out, azf_in, azf_sem)
     ax = wide_ax(state, low.at[0], high.at[0], ax_sem.at[0])
     axf = wide_ax(flags, flow, fhigh, axf_sem)
+    radial_terms(state, rate)
     pl.semaphore_wait(barrier, 65)
     start_ax(rows)
     start_all(ends)
@@ -713,7 +719,7 @@
     def own_marks(r):
         return marks[1, 16 * r : 16 * r + 16, :]
 
-    near_azimuthal(own_state, own_marks, 0, near_rate)
+    near_azimuthal(own_state, own_marks, near_rate, apart, copies)
     came_ax(rows)
     came_ax(mark_rows)
 
@@ -759,8 +765,9 @@
         outer_rows(0),
         ghost_row(0),
         mark_list(),
-        0,
         near_rate,
+        apart,
+        copies,
         near_first,
     )
     spread(send.at[0], recv.at[0], me, peers, go_sem.at[0, 0], go_sem.at[0, 1])
@@ -850,37 +857,37 @@
         lines[7, pl.ds(me, 1)] = outer_out[pl.ds(level, 1)]
 
     pl.when(is_last)(keep_outer)
-    stage(first, az_out, 5)
-    az = along_az(az_out, az_in.at[1], az_sem.at[1])
-    start_all(az)
     arrived(recv.at[0], go_sem.at[0, 1])
     project(recv.at[0], back.at[0], me, fwd, inv, twiddle, mix_high, mix_low)
 
-    column = 16 * (x // 2) + z
+    column = 32 * y + z
     meets = []
     for step in range(1, 4):
         over, under = level + step, level + 4 - step
         to_row, to_level = row + over // 4, lax.rem(over, 4)
-        to = 32 * lax.rem(to_level, 2) + 8 * (to_level // 2) + column
+        to = 8 * to_level + column
         item = copy(back.at[0], lines.at[3 - step], line_sem, 3 - step, ax=to_row, az=to)
         has_over, has_under = (row < 3) | (over < 4), (row > 0) | (under >= 4)
         meets.append((item, has_over, has_under))
         to_row, to_level = row - 1 + under // 4, lax.rem(under, 4)
-        to = 32 * lax.rem(to_level, 2) + 8 * (to_level // 2) + column
+        to = 8 * to_level + column
         item = copy(back.at[0], lines.at[2 + step], line_sem, 2 + step, ax=to_row, az=to)
         meets.append((item, has_under, has_over))
-    base = 32 * lax.rem(level, 2) + 8 * (level // 2)
+    base = 8 * level
     ahead, behind = cycle + 1, cycle + 15
-    to = base + 16 * (ahead // 8) + lax.rem(ahead, 8)
+    to = base + 32 * (ahead // 8) + lax.rem(ahead, 8)
     item = copy(back.at[0], lines.at[6], line_sem, 6, az=to)
     not_first, not_last = jnp.logical_not(is_first), jnp.logical_not(is_last)
     meets.append((item, not_last, not_first))
     behind = lax.rem(behind, 16)
-    to = base + 16 * (behind // 8) + lax.rem(behind, 8)
+    to = base + 32 * (behind // 8) + lax.rem(behind, 8)
     item = copy(back.at[0], lines.at[7], line_sem, 7, az=to)
     meets.append((item, not_first, not_last))
     for item, sends, _ in meets:
         pl.when(sends)(item.start)
+    stage(first, az_out, 5)
+    az = along_az(az_out, az_in.at[1], az_sem.at[1])
+    start_all(az)
 
     def hand_rim():
         for to in peers:
@@ -898,6 +905,7 @@
 
     pl.when(is_first)(mirror)
     arrived(extra_in, extra_sem.at[1])
+    line_alone(back.at[0], extra_in, cycle, near_rate, apart, copies)
     for item, _, comes in meets:
         pl.when(comes)(item.wait_recv)
     pl.when(is_last)(lambda: arrived(lines.at[7], outer_sem.at[1, 0]))
@@ -915,7 +923,7 @@
         pl.when((row == 3) & (level == 3 - r))(clamp_high)
     ax2 = wide_ax(first, low.at[1], high.at[1], ax_sem.at[1])
     start_ax(ax2)
-    line_rates(back.at[0], lines, extra_in, cycle, recv.at[1], apart, copies)
+    line_rates(back.at[0], lines, extra_in, near_rate, recv.at[1], apart, copies)
     project(recv.at[1], back.at[1], me, fwd, inv, twiddle, mix_high, mix_low)
     spread(back.at[1], ret, me, peers, come_sem.at[0], come_sem.at[1])
 
@@ -924,11 +932,7 @@
     came_all(az)
     sent_all(az)
     fill_az(1)
-    azimuthal(padded, padded_flags, 1, rate)
     sent_ax(ax2)
-    came_ax(ax2)
-    rims(first, 1)
-
     def rim_but_own():
         part = rim_in.at[pl.ds(0, 3)]
         pltpu.make_async_copy(part, part, rim_sem.at[1, 0]).wait()
@@ -940,6 +944,11 @@
     for r in range(4):
         for v in range(5):
             first[v, r] = jnp.where(lane40 == 15, block(v, r - 15)[3:43], first[v, r])
+
+    radial_terms(first, rate)
+    azimuthal(padded, padded_flags, 1, rate)
+    came_ax(ax2)
+    rims(first, 1)
 
     def combine_second(v, r, rows, here, slope):
         second[v, r, rows, :] = state[v, r, rows, :] * 0.75 + (here + slope * time_step) * 0.25

time: 44.5 us -> 44 us (0.989)
  no operation moved by 1% of the time
where the time goes in v6:
time: 44 us; the launch traced here: 43.9 us
  Pallas kernels  43 us (98%)
  other arithmetic  0.8 us (2%)
    pallas_call x1, Pallas kernels, local(): pl.pallas_call(kernel, out_shape=jax.ShapeDtypeStruct(state.shape, f32),...  43 us

profile of v6, /device:TPU:1, one launch (start us, length us, event | category | flops | bytes accessed | tf_op | source)
XLA Modules:
  0.0 43.9 jit_solution(9012686148495930662)
XLA Ops:
  0.0 0.0 copy-start
  0.0 43.0 %shard_map.64 = f32[5,4,40,128]{3,2,1,0:T(8,128)S(1)} custom-call(f32[5,4,40,128]{3,2,1,0:T(8,128)} %state_hbm.1, s32[2,4,40,128]{3,2,1,0:T(8,128)} %flags_hbm.1, bf16[2,80,64]{2,1,0:T(8,128)(2,1)} %constant.20.fwd_hbm, bf16[2,64,80]{2,1,0:T(8,128)(2,1)} %constant.27.inv_hbm, f32[4,40,256]{2,1,0:T(8,128)} %constant.10.clone.twiddle_hbm, ...), custom_call_target="tpu_custom_call" | custom-call | tf_op jit(solution)/shard_map/pallas_call | solution.py:986
  43.1 0.0 copy-done
  43.1 0.8 %sub.11 = f32[5,4,40,128]{3,2,1,0:T(8,128)} subtract(f32[5,4,40,128]{3,2,1,0:T(8,128)S(1)} %shard_map.64, f32[5,4,40,128]{3,2,1,0:T(8,128)S(1)} %copy-done) | non-fusion elementwise | flops 102400 | bytes 1228800 | tf_op jit(solution)/shard_map/sub | solution.py:1059
Async XLA Ops:
  0.0 43.1 %copy-start = (f32[5,4,40,128]{3,2,1,0:T(8,128)S(1)}, f32[5,4,40,128]{3,2,1,0:T(8,128)}, u32[]{:S(2)}) copy-start(f32[5,4,40,128]{3,2,1,0:T(8,128)} %state_hbm.1) | copy-start | bytes 1228804

commit v7 on v6

--- a/solution.py
+++ b/solution.py
@@ -257,7 +257,7 @@
                 combine(v, r, at8, u[v].cells[3 + r], slope)
         return carry
 
-    lax.fori_loop(0, 5, chunk, 0)
+    lax.fori_loop(0, 5, chunk, 0, unroll=5)
 
 
 def cell_of(width):
@@ -692,10 +692,10 @@
     axf = wide_ax(flags, flow, fhigh, axf_sem)
     radial_terms(state, rate)
     pl.semaphore_wait(barrier, 65)
+    start_all(ends)
+    start_all(mark_ends)
+    ghost.start()
     start_ax(rows)
-    start_all(ends)
-    ghost.start()
-    start_all(mark_ends)
     start_ax(mark_rows)
     start_all(az)
     start_all(azf)

time: 44 us -> 43.9 us (level)
  no operation moved by 1% of the time
where the time goes in v7:
time: 43.9 us; the launch traced here: 43.8 us
  Pallas kernels  43 us (98%)
  other arithmetic  0.8 us (2%)
    pallas_call x1, Pallas kernels, local(): pl.pallas_call(kernel, out_shape=jax.ShapeDtypeStruct(state.shape, f32),...  43 us

profile of v7, /device:TPU:1, one launch (start us, length us, event | category | flops | bytes accessed | tf_op | source)
XLA Modules:
  0.0 43.8 jit_solution(18419494345856196466)
XLA Ops:
  0.0 0.0 copy-start
  0.0 43.0 %shard_map.64 = f32[5,4,40,128]{3,2,1,0:T(8,128)S(1)} custom-call(f32[5,4,40,128]{3,2,1,0:T(8,128)} %state_hbm.1, s32[2,4,40,128]{3,2,1,0:T(8,128)} %flags_hbm.1, bf16[2,80,64]{2,1,0:T(8,128)(2,1)} %constant.20.fwd_hbm, bf16[2,64,80]{2,1,0:T(8,128)(2,1)} %constant.27.inv_hbm, f32[4,40,256]{2,1,0:T(8,128)} %constant.10.clone.twiddle_hbm, ...), custom_call_target="tpu_custom_call" | custom-call | tf_op jit(solution)/shard_map/pallas_call | solution.py:986
  43.0 0.0 copy-done
  43.0 0.8 %sub.11 = f32[5,4,40,128]{3,2,1,0:T(8,128)} subtract(f32[5,4,40,128]{3,2,1,0:T(8,128)S(1)} %shard_map.64, f32[5,4,40,128]{3,2,1,0:T(8,128)S(1)} %copy-done) | non-fusion elementwise | flops 102400 | bytes 1228800 | tf_op jit(solution)/shard_map/sub | solution.py:1059
Async XLA Ops:
  0.0 43.0 %copy-start = (f32[5,4,40,128]{3,2,1,0:T(8,128)S(1)}, f32[5,4,40,128]{3,2,1,0:T(8,128)}, u32[]{:S(2)}) copy-start(f32[5,4,40,128]{3,2,1,0:T(8,128)} %state_hbm.1) | copy-start | bytes 1228804
